TPU v7x, 32 devices: a whole 2x2x4 slice. The times are simulated.
32 devices in a mesh: wide: 4 (over z), context: 4 (over x, core), tensor: 2 (over y).
Axes of the slice: x: 2, y: 2, z: 4, core: 2. Of those that a mesh axis runs over, the one named last changes fastest.
Arguments:
- tokens: bfloat16 [12288, 2048], P(('wide', 'context')), may hold values from -6 to 6
- segment_of: int32 [12288], P('wide'), may hold values from 0 to 12, as said below
- parent_of: int32 [52], P('wide'), may hold values from 0 to 12, as said below
- valid: int32 [12288], P('wide'), may hold values from 0 to 1, as said below
- positions: int32 [12288], P(('wide', 'context')), may hold values from 0 to 1279, as said below
- g_attn: bfloat16 [2048], P('wide'), may hold values from 0.25 to 1.75
- w_q: bfloat16 [2048, 2048], P('wide', 'tensor'), may hold values from -0.125 to 0.125
- key_projection: bfloat16 [2048, 1024], P('wide', 'tensor'), may hold values from -0.125 to 0.125
- value_projection: bfloat16 [2048, 1024], P('wide', 'tensor'), may hold values from -0.125 to 0.125
- w_g: bfloat16 [2048, 16], P('wide', 'tensor'), may hold values from -0.125 to 0.125
- q_gain: bfloat16 [128], replicated, may hold values from 0.25 to 1.75
- k_gain: bfloat16 [128], replicated, may hold values from 0.25 to 1.75
- w_o: bfloat16 [2048, 2048], P('tensor', 'wide'), may hold values from -1 to 1
- g_mlp: bfloat16 [2048], P('wide'), may hold values from 0.25 to 1.75
- w_gate: bfloat16 [2048, 6144], P('wide', 'tensor'), may hold values from -0.125 to 0.125
- w_up: bfloat16 [2048, 6144], P('wide', 'tensor'), may hold values from -0.125 to 0.125
- w_down: bfloat16 [6144, 2048], P('tensor', 'wide'), may hold values from -0.078125 to 0.078125
- cotangent: bfloat16 [12288, 2048], P(('wide', 'context')), may hold values from -6 to 6
Outputs:
- layer_out: bfloat16 [12288, 2048], P(('wide', 'context'))
- grad_tokens: float32 [12288, 2048], P(('wide', 'context'))
- grad_g_attn: float32 [2048], P('wide')
- grad_w_q: float32 [2048, 2048], P('wide', 'tensor')
- grad_w_k: float32 [2048, 1024], P('wide', 'tensor')
- grad_w_v: float32 [2048, 1024], P('wide', 'tensor')
- grad_w_g: float32 [2048, 16], P('wide', 'tensor')
- grad_q_gain: float32 [128], replicated
- grad_k_gain: float32 [128], replicated
- grad_w_o: float32 [2048, 2048], P('tensor', 'wide')
- grad_g_mlp: float32 [2048], P('wide')
- grad_w_gate: float32 [2048, 6144], P('wide', 'tensor')
- grad_w_up: float32 [2048, 6144], P('wide', 'tensor')
- grad_w_down: float32 [6144, 2048], P('tensor', 'wide')
Inputs may be any that keep to these rules, and one draw needn't show every extreme that they name: `segment_of`: each group of 3072 tokens holds 1 tree and one block of 512 padding tokens. A tree is a trunk of 1024 tokens, 4 branches of 128 tokens, and 2 leaves of 128 tokens for each branch. Every trunk, branch and leaf is a run of consecutive tokens with a number of its own, and it lies after its parent. The segments of different trees and the padding block may lie between one another. In each group, one tree's trunk starts at the group's first token and one of its leaves ends at the group's last. The padding block lies between segments and has number 0. `parent_of`: entry s of a group's 13 entries is the segment that segment s hangs from; a trunk hangs from itself. `valid`: 1 on the trees' tokens, 0 on the padding block. `positions`: A token's place along its root-to-leaf path: trunk tokens count from 0, a branch continues from 1024, a leaf from 1152; padding has 0.
All inputs are finite; a program needn't handle non-finite values.
Results may differ from a plain program's by a relative error of at most 0.02.
Values may be sent and summed in bfloat16 or wider, within the bound.
No kernel may reach another device: no remote copies, remote signals or barrier semaphores. Data moves between devices by JAX's collectives and lax.ppermute only.
A program may use at most 256 MiB of HBM per device.

v0:
```python
import jax
import jax.numpy as jnp
from jax import lax
from jax.sharding import PartitionSpec as P

EPSILON = 1e-06
ROPE_BASE = 1000000.0


def product(left, right):
    return jnp.dot(left, right, preferred_element_type=jnp.float32)


def product_left(left, right):
    return lax.dot_general(
        left, right, (((0,), (0,)), ((), ())), preferred_element_type=jnp.float32
    )


def product_right(left, right):
    return lax.dot_general(
        left, right, (((1,), (1,)), ((), ())), preferred_element_type=jnp.float32
    )


def rms_scale(values, gain):
    return values * lax.rsqrt(jnp.mean(values * values, axis=-1, keepdims=True) + EPSILON) * gain


def rope_tables(positions, head_width):
    half_width = head_width // 2
    frequency = ROPE_BASE ** (-(jnp.arange(half_width, dtype=jnp.float32) * 2.0 / head_width))
    angles = positions.astype(jnp.float32)[:, None] * frequency[None, :]
    cosine_table = jnp.concatenate([jnp.cos(angles), jnp.cos(angles)], axis=-1)
    sine_table = jnp.concatenate([jnp.sin(angles), jnp.sin(angles)], axis=-1)
    return (cosine_table, sine_table)


def rotate(values, cosine_table, sine_table):
    half_width = values.shape[-1] // 2
    turned = jnp.concatenate([-values[..., half_width:], values[..., :half_width]], axis=-1)
    return values * cosine_table[:, None, :] + turned * sine_table[:, None, :]


def head_prep(linear, gain, cosine_table, sine_table):
    heads = linear.reshape(linear.shape[0], -1, gain.shape[0])
    return rotate(rms_scale(heads, gain), cosine_table, sine_table)


def norm_backward(values, gain, incoming):
    norm_value, norm_pull = jax.vjp(rms_scale, values, gain)
    return norm_pull(incoming)


def path_mask(tree_rows, key_rows, first_row, key_count):
    rows_per_block = tree_rows.shape[0]
    on_path = product_right(tree_rows, key_rows) > 0.5
    query_index = first_row + jnp.arange(rows_per_block, dtype=jnp.int32)
    key_index = jnp.arange(key_count, dtype=jnp.int32)
    earlier = key_index[None, :] < query_index[:, None]
    diagonal = key_index[None, :] == query_index[:, None]
    return on_path & earlier | diagonal


def block_scores(q_block, key_head, allowed, scale):
    scores = (
        jnp.einsum("qrd,kd->qrk", q_block, key_head, preferred_element_type=jnp.float32) * scale
    )
    return jnp.where(allowed[:, None, :], scores, -1e30)


def attend_forward(q_block, key_head, value_head, allowed, scale):
    scores = block_scores(q_block, key_head, allowed, scale)
    row_max = jnp.max(scores, axis=-1, keepdims=True)
    weights = jnp.exp(scores - row_max)
    row_sum = jnp.sum(weights, axis=-1, keepdims=True)
    probs = (weights / row_sum).astype(jnp.bfloat16)
    result = jnp.einsum("qrk,kd->qrd", probs, value_head, preferred_element_type=jnp.float32)
    return (result, (row_max + jnp.log(row_sum))[..., 0])


def attend_backward(q_block, key_head, value_head, grad_block, log_sum, allowed, scale):
    scores = block_scores(q_block, key_head, allowed, scale)
    probs = jnp.exp(scores - log_sum[..., None])
    grad_probs = jnp.einsum(
        "qrd,kd->qrk", grad_block, value_head, preferred_element_type=jnp.float32
    )
    inner = jnp.sum(probs * grad_probs, axis=-1, keepdims=True)
    grad_scores = (probs * (grad_probs - inner)).astype(jnp.bfloat16)
    grad_query = (
        jnp.einsum("qrk,kd->qrd", grad_scores, key_head, preferred_element_type=jnp.float32) * scale
    )
    grad_key = (
        jnp.einsum("qrk,qrd->kd", grad_scores, q_block, preferred_element_type=jnp.float32) * scale
    )
    grad_value = jnp.einsum(
        "qrk,qrd->kd", probs.astype(jnp.bfloat16), grad_block, preferred_element_type=jnp.float32
    )
    return (grad_query, grad_key, grad_value)


def shards(
    tokens,
    segment_of,
    parent_of,
    valid,
    positions,
    g_attn,
    w_q,
    key_projection,
    value_projection,
    w_g,
    q_gain,
    k_gain,
    w_o,
    g_mlp,
    w_gate,
    w_up,
    w_down,
    cotangent,
):
    row_count = tokens.shape[0]
    head_width = q_gain.shape[0]
    rows_per_group = segment_of.shape[0]
    seg_count = parent_of.shape[0]
    scale = head_width ** (-0.5)
    share_rows = row_count // lax.axis_size("tensor")
    share_first = lax.axis_index("tensor") * share_rows
    query_weight, key_weight, value_weight, gate_weight, attn_gain, out_weight = (
        lax.all_gather(w_q, "wide", axis=0, tiled=True),
        lax.all_gather(key_projection, "wide", axis=0, tiled=True),
        lax.all_gather(value_projection, "wide", axis=0, tiled=True),
        lax.all_gather(w_g, "wide", axis=0, tiled=True),
        lax.all_gather(g_attn, "wide", axis=0, tiled=True),
        lax.all_gather(w_o, "wide", axis=1, tiled=True),
    )
    gate_mlp_weight, up_weight, mlp_gain, down_weight = (
        lax.all_gather(w_gate, "wide", axis=0, tiled=True),
        lax.all_gather(w_up, "wide", axis=0, tiled=True),
        lax.all_gather(g_mlp, "wide", axis=0, tiled=True),
        lax.all_gather(w_down, "wide", axis=1, tiled=True),
    )
    tokens_f = tokens.astype(jnp.float32)
    tokens_share = lax.dynamic_slice_in_dim(tokens_f, share_first, share_rows)
    attn_gain_f = attn_gain.astype(jnp.float32)
    mlp_gain_f = mlp_gain.astype(jnp.float32)
    query_gain = q_gain.astype(jnp.float32)
    key_gain = k_gain.astype(jnp.float32)
    cosine_table, sine_table = rope_tables(positions, head_width)
    normed = rms_scale(tokens_f, attn_gain_f).astype(jnp.bfloat16)
    query_proj = product(normed, query_weight)
    key_proj = product(normed, key_weight)
    value_proj = product(normed, value_weight)
    gate_proj = product(normed, gate_weight)
    query_rot = head_prep(query_proj, query_gain, cosine_table, sine_table).astype(jnp.bfloat16)
    key_rot = head_prep(key_proj, key_gain, cosine_table, sine_table).astype(jnp.bfloat16)
    head_count = query_rot.shape[1]
    kv_count = key_rot.shape[1]
    head_repeat = head_count // kv_count
    keys_all, values_all = (
        lax.all_gather(
            key_rot.reshape(row_count, kv_count * head_width), "context", axis=0, tiled=True
        ),
        lax.all_gather(value_proj.astype(jnp.bfloat16), "context", axis=0, tiled=True),
    )
    seg_index = jnp.arange(seg_count, dtype=jnp.int32)
    single = (parent_of[:, None] == seg_index[None, :]).astype(jnp.float32)
    lookup_table = jnp.minimum(
        jnp.eye(seg_count, dtype=jnp.float32) + single + product(single, single), 1.0
    )
    live_all = valid.astype(jnp.float32)
    key_rows = (segment_of[:, None] == seg_index[None, :]).astype(jnp.float32) * live_all[:, None]
    own_first = lax.axis_index("context") * row_count
    own_seg = lax.dynamic_slice_in_dim(segment_of, own_first, row_count)
    own_live = lax.dynamic_slice_in_dim(live_all, own_first, row_count)
    tree_rows = (
        product((own_seg[:, None] == seg_index[None, :]).astype(jnp.float32), lookup_table)
        * own_live[:, None]
    )
    rows_per_block = min(256, row_count)
    count_of_blocks = row_count // rows_per_block
    tree_blocks = tree_rows.reshape(count_of_blocks, rows_per_block, seg_count)
    block_firsts = own_first + jnp.arange(count_of_blocks, dtype=jnp.int32) * rows_per_block
    query_heads = query_rot.reshape(
        count_of_blocks, rows_per_block, kv_count, head_repeat, head_width
    ).transpose(2, 0, 1, 3, 4)
    key_heads = keys_all.reshape(rows_per_group, kv_count, head_width).transpose(1, 0, 2)
    value_heads = values_all.reshape(rows_per_group, kv_count, head_width).transpose(1, 0, 2)

    def head_forward(pieces):
        query_head, key_head, value_head = pieces

        def block_forward(block_pieces):
            q_block, tree_block, first_row = block_pieces
            allowed = path_mask(tree_block, key_rows, first_row, rows_per_group)
            return attend_forward(q_block, key_head, value_head, allowed, scale)

        return lax.map(block_forward, (query_head, tree_blocks, block_firsts))

    attended_heads, log_sums = lax.map(head_forward, (query_heads, key_heads, value_heads))
    attended_rows = attended_heads.transpose(1, 2, 0, 3, 4).reshape(
        row_count, head_count, head_width
    )
    gate_sig = jax.nn.sigmoid(gate_proj)
    gated = (
        (attended_rows * gate_sig[:, :, None])
        .reshape(row_count, head_count * head_width)
        .astype(jnp.bfloat16)
    )
    attn_terms = product(gated, out_weight)
    middle = tokens_f + lax.psum(attn_terms, "tensor")
    middle_share = lax.dynamic_slice_in_dim(middle, share_first, share_rows)
    normed_mlp = rms_scale(middle, mlp_gain_f).astype(jnp.bfloat16)
    gate_mlp = product(normed_mlp, gate_mlp_weight)
    up_mlp = product(normed_mlp, up_weight)
    mixed = (jax.nn.silu(gate_mlp) * up_mlp).astype(jnp.bfloat16)
    mlp_terms = product(mixed, down_weight)
    layer_out = (
        middle + lax.psum(mlp_terms.astype(jnp.bfloat16), "tensor").astype(jnp.float32)
    ).astype(jnp.bfloat16)
    grad_down = product_left(mixed, cotangent)
    grad_mixed = product_right(cotangent, down_weight)
    sig_mlp = jax.nn.sigmoid(gate_mlp)
    grad_gate_low = (grad_mixed * up_mlp * sig_mlp * (1.0 + gate_mlp * (1.0 - sig_mlp))).astype(
        jnp.bfloat16
    )
    grad_up_low = (grad_mixed * gate_mlp * sig_mlp).astype(jnp.bfloat16)
    grad_gate_w = product_left(normed_mlp, grad_gate_low)
    grad_up_w = product_left(normed_mlp, grad_up_low)
    grad_normed_share = lax.psum_scatter(
        product_right(grad_gate_low, gate_mlp_weight) + product_right(grad_up_low, up_weight),
        "tensor",
        scatter_dimension=0,
        tiled=True,
    )
    grad_middle_norm, grad_mlp_gain = norm_backward(middle_share, mlp_gain_f, grad_normed_share)
    cot_share = lax.dynamic_slice_in_dim(cotangent, share_first, share_rows).astype(jnp.float32)
    grad_middle_share = cot_share + grad_middle_norm
    grad_attn_share = grad_middle_share.astype(jnp.bfloat16)
    grad_attn_low = lax.all_gather(grad_attn_share, "tensor", axis=0, tiled=True)
    grad_out_w = product_left(gated, grad_attn_low)
    grad_gated = product_right(grad_attn_low, out_weight).reshape(row_count, head_count, head_width)
    grad_attended = (grad_gated * gate_sig[:, :, None]).astype(jnp.bfloat16)
    grad_head_gate = (
        jnp.sum(grad_gated * attended_rows, axis=-1) * gate_sig * (1.0 - gate_sig)
    ).astype(jnp.bfloat16)
    grad_heads = grad_attended.reshape(
        count_of_blocks, rows_per_block, kv_count, head_repeat, head_width
    ).transpose(2, 0, 1, 3, 4)

    def head_backward(pieces):
        query_head, key_head, value_head, grad_head, log_head = pieces

        def block_backward(running, block_pieces):
            q_block, grad_block, log_block, tree_block, first_row = block_pieces
            allowed = path_mask(tree_block, key_rows, first_row, rows_per_group)
            grad_query, grad_key, grad_value = attend_backward(
                q_block, key_head, value_head, grad_block, log_block, allowed, scale
            )
            return ((running[0] + grad_key, running[1] + grad_value), grad_query)

        empty_sum = jnp.zeros((rows_per_group, head_width), jnp.float32)
        key_value_sums, grad_queries = lax.scan(
            block_backward,
            (empty_sum, empty_sum),
            (query_head, grad_head, log_head, tree_blocks, block_firsts),
        )
        return (grad_queries, key_value_sums[0], key_value_sums[1])

    grad_query_heads, grad_key_heads, grad_value_heads = lax.map(
        head_backward, (query_heads, key_heads, value_heads, grad_heads, log_sums)
    )
    grad_keys_all = grad_key_heads.transpose(1, 0, 2).reshape(rows_per_group, kv_count * head_width)
    grad_values_all = grad_value_heads.transpose(1, 0, 2).reshape(
        rows_per_group, kv_count * head_width
    )
    grad_keys, grad_values = (
        lax.psum_scatter(
            grad_keys_all.astype(jnp.bfloat16), "context", scatter_dimension=0, tiled=True
        ).astype(jnp.float32),
        lax.psum_scatter(
            grad_values_all.astype(jnp.bfloat16), "context", scatter_dimension=0, tiled=True
        ).astype(jnp.float32),
    )
    grad_query_rot = grad_query_heads.transpose(1, 2, 0, 3, 4).reshape(
        row_count, head_count, head_width
    )

    def rope_piece(linear, gain):
        return head_prep(linear, gain, cosine_table, sine_table)

    query_value, query_pull = jax.vjp(rope_piece, query_proj, query_gain)
    grad_query_proj, grad_query_gain = query_pull(grad_query_rot)
    key_value, key_pull = jax.vjp(rope_piece, key_proj, key_gain)
    grad_key_proj, grad_key_gain = key_pull(grad_keys.reshape(row_count, kv_count, head_width))
    grad_query_low = grad_query_proj.astype(jnp.bfloat16)
    grad_key_low = grad_key_proj.astype(jnp.bfloat16)
    grad_value_low = grad_values.astype(jnp.bfloat16)
    grad_query_w = product_left(normed, grad_query_low)
    grad_key_w = product_left(normed, grad_key_low)
    grad_value_w = product_left(normed, grad_value_low)
    grad_head_gate_w = product_left(normed, grad_head_gate)
    grad_normed_attn = lax.psum_scatter(
        (
            product_right(grad_query_low, query_weight)
            + product_right(grad_key_low, key_weight)
            + product_right(grad_value_low, value_weight)
            + product_right(grad_head_gate, gate_weight)
        ).astype(jnp.bfloat16),
        "tensor",
        scatter_dimension=0,
        tiled=True,
    ).astype(jnp.float32)
    grad_tokens_norm, grad_attn_gain = norm_backward(tokens_share, attn_gain_f, grad_normed_attn)
    grad_tokens = lax.all_gather(
        (grad_middle_share + grad_tokens_norm).astype(jnp.bfloat16), "tensor", axis=0, tiled=True
    ).astype(jnp.float32)
    sum_query_gain, sum_key_gain, sum_attn_gain, sum_mlp_gain = lax.psum(
        (grad_query_gain, grad_key_gain, grad_attn_gain, grad_mlp_gain),
        ("wide", "context", "tensor"),
    )
    gain_piece = sum_attn_gain.shape[0] // lax.axis_size("wide")
    gain_first = lax.axis_index("wide") * gain_piece
    final_attn_gain = lax.dynamic_slice_in_dim(sum_attn_gain, gain_first, gain_piece)
    final_mlp_gain = lax.dynamic_slice_in_dim(sum_mlp_gain, gain_first, gain_piece)
    (
        share_query,
        share_key,
        share_value,
        share_head_gate,
        share_out,
        share_gate,
        share_up,
        share_down,
    ) = (
        lax.psum_scatter(
            grad_query_w.astype(jnp.bfloat16), "wide", scatter_dimension=0, tiled=True
        ).astype(jnp.float32),
        lax.psum_scatter(
            grad_key_w.astype(jnp.bfloat16), "wide", scatter_dimension=0, tiled=True
        ).astype(jnp.float32),
        lax.psum_scatter(
            grad_value_w.astype(jnp.bfloat16), "wide", scatter_dimension=0, tiled=True
        ).astype(jnp.float32),
        lax.psum_scatter(
            grad_head_gate_w.astype(jnp.bfloat16), "wide", scatter_dimension=0, tiled=True
        ).astype(jnp.float32),
        lax.psum_scatter(
            grad_out_w.astype(jnp.bfloat16), "wide", scatter_dimension=1, tiled=True
        ).astype(jnp.float32),
        lax.psum_scatter(
            grad_gate_w.astype(jnp.bfloat16), "wide", scatter_dimension=0, tiled=True
        ).astype(jnp.float32),
        lax.psum_scatter(
            grad_up_w.astype(jnp.bfloat16), "wide", scatter_dimension=0, tiled=True
        ).astype(jnp.float32),
        lax.psum_scatter(
            grad_down.astype(jnp.bfloat16), "wide", scatter_dimension=1, tiled=True
        ).astype(jnp.float32),
    )
    (
        final_query,
        final_key,
        final_value,
        final_head_gate,
        final_out,
        final_gate,
        final_up,
        final_down,
    ) = (
        lax.psum(share_query.astype(jnp.bfloat16), "context").astype(jnp.float32),
        lax.psum(share_key.astype(jnp.bfloat16), "context").astype(jnp.float32),
        lax.psum(share_value.astype(jnp.bfloat16), "context").astype(jnp.float32),
        lax.psum(share_head_gate.astype(jnp.bfloat16), "context").astype(jnp.float32),
        lax.psum(share_out.astype(jnp.bfloat16), "context").astype(jnp.float32),
        lax.psum(share_gate.astype(jnp.bfloat16), "context").astype(jnp.float32),
        lax.psum(share_up.astype(jnp.bfloat16), "context").astype(jnp.float32),
        lax.psum(share_down.astype(jnp.bfloat16), "context").astype(jnp.float32),
    )
    return (
        layer_out,
        grad_tokens,
        final_attn_gain,
        final_query,
        final_key,
        final_value,
        final_head_gate,
        sum_query_gain,
        sum_key_gain,
        final_out,
        final_mlp_gain,
        final_gate,
        final_up,
        final_down,
    )


def solution(mesh):
    placed = (
        P(("wide", "context"), None),
        P("wide"),
        P("wide"),
        P("wide"),
        P(("wide", "context")),
        P("wide"),
        P("wide", "tensor"),
        P("wide", "tensor"),
        P("wide", "tensor"),
        P("wide", "tensor"),
        P(),
        P(),
        P("tensor", "wide"),
        P("wide"),
        P("wide", "tensor"),
        P("wide", "tensor"),
        P("tensor", "wide"),
        P(("wide", "context"), None),
    )
    return jax.shard_map(
        shards,
        mesh=mesh,
        in_specs=placed,
        out_specs=(
            P(("wide", "context"), None),
            P(("wide", "context"), None),
            P("wide"),
            P("wide", "tensor"),
            P("wide", "tensor"),
            P("wide", "tensor"),
            P("wide", "tensor"),
            P(),
            P(),
            P("tensor", "wide"),
            P("wide"),
            P("wide", "tensor"),
            P("wide", "tensor"),
            P("tensor", "wide"),
        ),
        check_vma=False,
    )
```

profile of v0, /device:TPU:0, one launch (start us, length us, event | category | flops | bytes accessed | tf_op | source)
XLA Modules:
  0.0 3120.8 jit_solution(3230142218742291596)
XLA Ops:
  64.6 39.9 %all-gather.20.cloned.1.call-done = bf16[2048,512]{1,0:T(8,128)(2,1)} async-done(((bf16[512,512]{1,0:T(8,128)(2,1)}), bf16[2048,512]{1,0:T(8,128)(2,1)}) %all-gather.20.cloned.1.call-update) | async-done | bytes 2097168 | tf_op jit(solution)/shard_map/all_gather | solution.py:132
  131.8 54.3 %all-gather.14.cloned.1.call-done = bf16[2048,1024]{1,0:T(8,128)(2,1)} async-done(((bf16[512,1024]{1,0:T(8,128)(2,1)}), bf16[2048,1024]{1,0:T(8,128)(2,1)}) %all-gather.14.cloned.1.call-update) | async-done | bytes 4194320 | tf_op jit(solution)/shard_map/all_gather | solution.py:130
  249.8 115.0 %while.58 = (s32[]{:T(128)}, f32[4,3,256,2,128]{4,2,3,1,0:T(8,128)}, f32[4,3,256,2]{2,3,1,0:T(2,128)}, bf16[4,3,256,2,128]{4,2,3,1,0:T(8,128)(2,1)}, bf16[4,3072...) while((s32[]{:T(128)}, ...), condition=%wide.region_8.9_spmd.clone, body=%wide.region_3.8_spmd.clone.sunk | while | flops 848639744 | bytes 29728112 | solution.py:200
  398.6 139.2 %all-reduce.10.cloned.1.call-done = f32[768,2048]{1,0:T(8,128)} async-done(((f32[768,2048]{1,0:T(8,128)}), f32[768,2048]{1,0:T(8,128)}) %all-reduce.10.cloned.1.call-update) | async-done | bytes 6291472 | tf_op jit(solution)/shard_map/psum | solution.py:211
  548.0 209.7 %all-gather.26.cloned.1.call-done = bf16[2048,3072]{1,0:T(8,128)(2,1)} async-done(((bf16[512,3072]{1,0:T(8,128)(2,1)}), bf16[2048,3072]{1,0:T(8,128)(2,1)}) %all-gather.26.cloned.1.call-update) | async-done | bytes 12582928 | tf_op jit(solution)/shard_map/all_gather | solution.py:138
  772.9 202.9 %all-gather.28.cloned.1.call-done = bf16[2048,3072]{1,0:T(8,128)(2,1)} async-done(((bf16[512,3072]{1,0:T(8,128)(2,1)}), bf16[2048,3072]{1,0:T(8,128)(2,1)}) %all-gather.28.cloned.1.call-update) | async-done | bytes 12582928 | tf_op jit(solution)/shard_map/all_gather | solution.py:139
  991.8 202.0 %all-gather.30.cloned.1.call-done = bf16[3072,2048]{1,0:T(8,128)(2,1)} async-done(((bf16[3072,512]{1,0:T(8,128)(2,1)}), bf16[3072,2048]{1,0:T(8,128)(2,1)}) %all-gather.30.cloned.1.call-update) | async-done | bytes 12582928 | tf_op jit(solution)/shard_map/all_gather | solution.py:141
  1249.5 73.1 %reduce-scatter.13.cloned.1.call-done = f32[384,2048]{1,0:T(8,128)} async-done(((f32[768,2048]{1,0:T(8,128)}), f32[384,2048]{1,0:T(8,128)}) %reduce-scatter.13.cloned.1.call-update) | async-done | bytes 3145744 | tf_op jit(solution)/shard_map/reduce_scatter | solution.py:230
  1331.9 44.9 %all-gather.32.cloned.1.call-done = bf16[768,2048]{1,0:T(8,128)(2,1)} async-done(((bf16[384,2048]{1,0:T(8,128)(2,1)}), bf16[768,2048]{1,0:T(8,128)(2,1)}) %all-gather.32.cloned.1.call-update) | async-done | bytes 3145744 | tf_op jit(solution)/shard_map/all_gather | solution.py:240
  1391.1 292.8 %while.60 = (s32[]{:T(128)}, f32[4,3,256,2,128]{4,2,1,3,0:T(8,128)}, bf16[4,3072,128]{1,2,0:T(8,128)(2,1)}, bf16[4,3072,128]{1,2,0:T(8,128)(2,1)}, bf16[4,3,256,...) while((s32[]{:T(128)}, ...), condition=%wide.region_19.20_spmd.clone, body=%wide.region_15.19_spmd.clone.sunk | while | flops 2053912320 | bytes 136193936 | solution.py:270
  1394.5 63.5 %while.62 = (s32[]{:T(128)}, f32[3072,128]{1,0:T(8,128)}, f32[3072,128]{1,0:T(8,128)}, f32[3,256,2,128]{3,1,2,0:T(8,128)}, bf16[3,256,13]{1,2,0:T(8,128)(2,1)}, ...) while((s32[]{:T(128)}, f32[3072,128]{1,0:T(8,128)}, ...), condition=%wide.region_18.18_spmd.clone, body=%wide.region_16.17_spmd.clone.sunk | while | flops 2053832448 | bytes 118755376 | solution.py:263
  1467.7 63.5 %while.62 = (s32[]{:T(128)}, f32[3072,128]{1,0:T(8,128)}, f32[3072,128]{1,0:T(8,128)}, f32[3,256,2,128]{3,1,2,0:T(8,128)}, bf16[3,256,13]{1,2,0:T(8,128)(2,1)}, ...) while((s32[]{:T(128)}, f32[3072,128]{1,0:T(8,128)}, ...), condition=%wide.region_18.18_spmd.clone, body=%wide.region_16.17_spmd.clone.sunk | while | flops 2053832448 | bytes 118755376 | solution.py:263
  1540.9 63.5 %while.62 = (s32[]{:T(128)}, f32[3072,128]{1,0:T(8,128)}, f32[3072,128]{1,0:T(8,128)}, f32[3,256,2,128]{3,1,2,0:T(8,128)}, bf16[3,256,13]{1,2,0:T(8,128)(2,1)}, ...) while((s32[]{:T(128)}, f32[3072,128]{1,0:T(8,128)}, ...), condition=%wide.region_18.18_spmd.clone, body=%wide.region_16.17_spmd.clone.sunk | while | flops 2053832448 | bytes 118755376 | solution.py:263
  1614.1 63.5 %while.62 = (s32[]{:T(128)}, f32[3072,128]{1,0:T(8,128)}, f32[3072,128]{1,0:T(8,128)}, f32[3,256,2,128]{3,1,2,0:T(8,128)}, bf16[3,256,13]{1,2,0:T(8,128)(2,1)}, ...) while((s32[]{:T(128)}, f32[3072,128]{1,0:T(8,128)}, ...), condition=%wide.region_18.18_spmd.clone, body=%wide.region_16.17_spmd.clone.sunk | while | flops 2053832448 | bytes 118755376 | solution.py:263
  1731.1 31.4 %reduce-scatter.17.cloned.1.call-done = bf16[768,512]{0,1:T(8,128)(2,1)} async-done(((bf16[3072,512]{0,1:T(8,128)(2,1)}), bf16[768,512]{0,1:T(8,128)(2,1)}) %reduce-scatter.17.cloned.1.call-update) | async-done | bytes 786448 | tf_op jit(solution)/shard_map/reduce_scatter | solution.py:281
  1894.1 80.0 %reduce-scatter.21.cloned.1.call-done = bf16[512,1024]{1,0:T(8,128)(2,1)} async-done(((bf16[2048,1024]{1,0:T(8,128)(2,1)}), bf16[512,1024]{1,0:T(8,128)(2,1)}) %reduce-scatter.21.cloned.1.call-update) | async-done | bytes 1048592 | tf_op jit(solution)/shard_map/reduce_scatter | solution.py:336
  1974.1 214.7 %reduce-scatter.31.cloned.1.call-done = bf16[512,3072]{1,0:T(8,128)(2,1)} async-done(((bf16[2048,3072]{1,0:T(8,128)(2,1)}), bf16[512,3072]{1,0:T(8,128)(2,1)}) %reduce-scatter.31.cloned.1.call-update) | async-done | bytes 3145744 | tf_op jit(solution)/shard_map/reduce_scatter | solution.py:351
  2188.8 215.4 %reduce-scatter.33.cloned.1.call-done = bf16[512,3072]{1,0:T(8,128)(2,1)} async-done(((bf16[2048,3072]{1,0:T(8,128)(2,1)}), bf16[512,3072]{1,0:T(8,128)(2,1)}) %reduce-scatter.33.cloned.1.call-update) | async-done | bytes 3145744 | tf_op jit(solution)/shard_map/reduce_scatter | solution.py:354
  2404.3 215.3 %reduce-scatter.35.cloned.1.call-done = bf16[3072,512]{1,0:T(8,128)(2,1)} async-done(((bf16[3072,2048]{1,0:T(8,128)(2,1)}), bf16[3072,512]{1,0:T(8,128)(2,1)}) %reduce-scatter.35.cloned.1.call-update) | async-done | bytes 3145744 | tf_op jit(solution)/shard_map/reduce_scatter | solution.py:357
  2619.5 47.9 %reduce-scatter.23.cloned.1.call-done = bf16[512,512]{1,0:T(8,128)(2,1)} async-done(((bf16[2048,512]{1,0:T(8,128)(2,1)}), bf16[512,512]{1,0:T(8,128)(2,1)}) %reduce-scatter.23.cloned.1.call-update) | async-done | bytes 524304 | tf_op jit(solution)/shard_map/reduce_scatter | solution.py:339
  2667.4 46.1 %reduce-scatter.25.cloned.1.call-done = bf16[512,512]{1,0:T(8,128)(2,1)} async-done(((bf16[2048,512]{1,0:T(8,128)(2,1)}), bf16[512,512]{1,0:T(8,128)(2,1)}) %reduce-scatter.25.cloned.1.call-update) | async-done | bytes 524304 | tf_op jit(solution)/shard_map/reduce_scatter | solution.py:342
  2713.5 88.0 %all-reduce.12.cloned.1.call-done = bf16[768,2048]{1,0:T(8,128)(2,1)} async-done(((bf16[768,2048]{1,0:T(8,128)(2,1)}), bf16[768,2048]{1,0:T(8,128)(2,1)}) %all-reduce.12.cloned.1.call-update) | async-done | bytes 3145744 | tf_op jit(solution)/shard_map/psum | solution.py:219
  2829.7 39.8 %all-reduce.4 = (f32[2048]{0:T(1024)S(1)}, f32[128]{0:T(128)}, f32[128]{0:T(128)}, f32[2048]{0:T(1024)S(1)}) all-reduce(f32[2048]{0:T(1024)S(1)} %get-tuple-element.497, f32[128]{0:T(128)S(1)} %copy-done.84, f32[128]{0:T(128)S(1)} %copy-done.85, ...), channel_id=1, replica_groups=mesh['wide'=4,'context'=4,'tensor'=2] {'wide','context','tensor'}, use_global_device_ids=true, to_apply=%region_29.30 | all-reduce | flops 4352 | bytes 34816 | tf_op jit(solution)/shard_map/psum | solution.py:318
  2876.3 219.7 %all-reduce.14.cloned.1.call-done = (bf16[512,1024]{1,0:T(8,128)(2,1)}, bf16[512,512]{1,0:T(8,128)(2,1)}, bf16[512,512]{1,0:T(8,128)(2,1)}, bf16[1024,512]{1,0:T...) async-done(((bf16[512,1024]{1,0:T(8,128)(2,1)}, bf16[512,512]{1,0:T(8,128)(2,1)}, bf16[512,512]{1,0:T(8,128)(2,1)}, ...) | async-done | bytes 12582928 | tf_op jit(solution)/shard_map/psum | solution.py:371
  (973 shorter events, 1035.1 us)
Async XLA Ops:
  7.9 96.6 %all-gather.20.cloned.1.call-start = ((), (), s32[]{:S(2)}) async-start(), calls=%async_computation.15 | async-start | bytes 2621440 | tf_op jit(solution)/shard_map/all_gather | solution.py:132
  8.7 177.4 %all-gather.14.cloned.1.call-start = ((), (), s32[]{:S(2)}) async-start(), calls=%async_computation.12 | async-start | bytes 5242880 | tf_op jit(solution)/shard_map/all_gather | solution.py:130
  9.4 216.2 %all-gather.18.cloned.1.call-start = ((), (), s32[]{:S(2)}) async-start(), calls=%async_computation.14 | async-start | bytes 3932160 | tf_op jit(solution)/shard_map/all_gather | solution.py:161
  64.6 181.2 %all-gather.22.cloned.1.call-start = ((), (), s32[]{:S(2)}) async-start(), calls=%async_computation.16 | async-start | bytes 3932160 | tf_op jit(solution)/shard_map/all_gather | solution.py:164
  108.9 267.6 %all-gather.24.cloned.1.call-start = ((), (), s32[]{:S(2)}) async-start(), calls=%async_computation.17 | async-start | bytes 5242880 | tf_op jit(solution)/shard_map/all_gather | solution.py:135
  109.4 428.4 %all-reduce.10.cloned.1.call-start = ((), (), s32[]{:S(2)}) async-start(), calls=%async_computation.18 | async-start | bytes 12582912 | tf_op jit(solution)/shard_map/psum | solution.py:211
  384.5 373.2 %all-gather.26.cloned.1.call-start = ((), (), s32[]{:S(2)}) async-start(), calls=%async_computation.19 | async-start | bytes 15728640 | tf_op jit(solution)/shard_map/all_gather | solution.py:138
  385.3 590.5 %all-gather.28.cloned.1.call-start = ((), (), s32[]{:S(2)}) async-start(), calls=%async_computation.20 | async-start | bytes 15728640 | tf_op jit(solution)/shard_map/all_gather | solution.py:139
  386.0 807.7 %all-gather.30.cloned.1.call-start = ((), (), s32[]{:S(2)}) async-start(), calls=%async_computation.21 | async-start | bytes 15728640 | tf_op jit(solution)/shard_map/all_gather | solution.py:141
  386.6 936.1 %reduce-scatter.13.cloned.1.call-start = ((), (), s32[]{:S(2)}) async-start(), calls=%async_computation.23 | async-start | bytes 9437184 | tf_op jit(solution)/shard_map/reduce_scatter | solution.py:230
  1247.3 129.5 %all-gather.32.cloned.1.call-start = ((), (), s32[]{:S(2)}) async-start(), calls=%async_computation.24 | async-start | bytes 4718592 | tf_op jit(solution)/shard_map/all_gather | solution.py:240
  1331.7 390.2 %reduce-scatter.15.cloned.1.call-start = ((), (), s32[]{:S(2)}) async-start(), calls=%async_computation.25 | async-start | bytes 3932160 | tf_op jit(solution)/shard_map/reduce_scatter | solution.py:278
  1684.4 183.8 %reduce-scatter.19.cloned.1.call-start = ((), (), s32[]{:S(2)}) async-start(), calls=%async_computation.27 | async-start | bytes 4718592 | tf_op jit(solution)/shard_map/reduce_scatter | solution.py:303
  1771.5 122.5 %reduce-scatter.29.cloned.1.call-start = ((), (), s32[]{:S(2)}) async-start(), calls=%async_computation.33 | async-start | bytes 5242880 | tf_op jit(solution)/shard_map/reduce_scatter | solution.py:348
  1780.1 194.1 %reduce-scatter.21.cloned.1.call-start = ((), (), s32[]{:S(2)}) async-start(), calls=%async_computation.29 | async-start | bytes 5242880 | tf_op jit(solution)/shard_map/reduce_scatter | solution.py:336
  1788.4 400.5 %reduce-scatter.31.cloned.1.call-start = ((), (), s32[]{:S(2)}) async-start(), calls=%async_computation.34 | async-start | bytes 15728640 | tf_op jit(solution)/shard_map/reduce_scatter | solution.py:351
  1804.3 599.9 %reduce-scatter.33.cloned.1.call-start = ((), (), s32[]{:S(2)}) async-start(), calls=%async_computation.35 | async-start | bytes 15728640 | tf_op jit(solution)/shard_map/reduce_scatter | solution.py:354
  1820.7 798.8 %reduce-scatter.35.cloned.1.call-start = ((), (), s32[]{:S(2)}) async-start(), calls=%async_computation.36 | async-start | bytes 15728640 | tf_op jit(solution)/shard_map/reduce_scatter | solution.py:357
  1836.8 830.6 %reduce-scatter.23.cloned.1.call-start = ((), (), s32[]{:S(2)}) async-start(), calls=%async_computation.30 | async-start | bytes 2621440 | tf_op jit(solution)/shard_map/reduce_scatter | solution.py:339
  1841.2 872.3 %reduce-scatter.25.cloned.1.call-start = ((), (), s32[]{:S(2)}) async-start(), calls=%async_computation.31 | async-start | bytes 2621440 | tf_op jit(solution)/shard_map/reduce_scatter | solution.py:342
  1845.8 955.8 %all-reduce.12.cloned.1.call-start = ((), (), s32[]{:S(2)}) async-start(), calls=%async_computation.22 | async-start | bytes 6291456 | tf_op jit(solution)/shard_map/psum | solution.py:219
  1861.2 962.0 %reduce-scatter.27.cloned.1.call-start = ((), (), s32[]{:S(2)}) async-start(), calls=%async_computation.32 | async-start | bytes 40960 | tf_op jit(solution)/shard_map/reduce_scatter | solution.py:345
  1868.2 1002.6 %all-gather.34.cloned.1.call-start = ((), (), s32[]{:S(2)}) async-start(), calls=%async_computation.28 | async-start | bytes 4718592 | tf_op jit(solution)/shard_map/all_gather | solution.py:315
  1877.3 1218.6 %all-reduce.14.cloned.1.call-start = ((), (), s32[]{:S(2)}) async-start(), calls=%async_computation.37 | async-start | bytes 25165824 | tf_op jit(solution)/shard_map/psum | solution.py:371
  (243 other events, 3932.5 us)
Sparse Core Ops, SparseCore 0:
  9.6 48.6 all-gather.15
  59.8 44.6 all-gather.19
  106.1 79.8 all-gather.13
  217.2 28.5 all-gather.21
  247.2 80.7 all-gather.23
  384.6 153.1 all-reduce.9
  539.5 218.1 all-gather.25
  759.4 216.3 all-gather.27
  977.3 216.3 all-gather.29
  1247.4 75.2 reduce-scatter.12
  1331.8 44.9 all-gather.31
  1684.0 37.9 reduce-scatter.14
  1724.5 37.9 reduce-scatter.16
  1771.7 43.3 reduce-scatter.18
  1817.3 76.7 reduce-scatter.28
  1896.8 77.2 reduce-scatter.20
  1976.4 212.3 reduce-scatter.30
  2191.3 212.8 reduce-scatter.32
  2406.6 212.8 reduce-scatter.34
  2622.5 44.8 reduce-scatter.22
  2670.3 43.1 reduce-scatter.24
  2716.5 85.0 all-reduce.11
  2825.4 44.4 all-gather.33
  2873.3 222.6 all-reduce.13
  (2 shorter events, 45.9 us)
where the time goes:
time: 3130 us; the launch traced here: 3120 us
  waiting for transfers between devices  2220 us (71%)
  matrix products  463 us (15%)
  local copies, waits for them, and re-layouts  174 us (6%)
  other arithmetic  159 us (5%)
  blocking collectives  84.7 us (3%)
    psum x1, waiting for transfers between devices, shards(): lax.psum(share_query.astype(jnp.bfloat16), 'context').astype(jnp.float32)  220 us
    reduce_scatter x1, waiting for transfers between devices, shards(): lax.psum_scatter(grad_up_w.astype(jnp.bfloat16), 'wide', scatter_dimensio...  215 us
    reduce_scatter x1, waiting for transfers between devices, shards(): lax.psum_scatter(grad_down.astype(jnp.bfloat16), 'wide', scatter_dimensio...  215 us
    reduce_scatter x1, waiting for transfers between devices, shards(): lax.psum_scatter(grad_gate_w.astype(jnp.bfloat16), 'wide', scatter_dimens...  215 us
    all_gather x1, waiting for transfers between devices, shards(): lax.all_gather(w_gate, 'wide', axis=0, tiled=True)  210 us
    all_gather x1, waiting for transfers between devices, shards(): lax.all_gather(w_up, 'wide', axis=0, tiled=True)  203 us
    all_gather x1, waiting for transfers between devices, shards(): lax.all_gather(w_down, 'wide', axis=1, tiled=True)  202 us
    psum x1, waiting for transfers between devices, shards(): middle = tokens_f + lax.psum(attn_terms, 'tensor')  139 us
  transfers between devices with their start and end apart: 26, of which 22 were waited for; matrix products, arithmetic and copies ran while one was open for 12% of the time, Pallas kernels for 0%

commit v1 on v0

--- a/solution.py
+++ b/solution.py
@@ -1,6 +1,10 @@
+import functools
+
 import jax
 import jax.numpy as jnp
 from jax import lax
+from jax.experimental import pallas as pl
+from jax.experimental.pallas import tpu as pltpu
 from jax.sharding import PartitionSpec as P
 
 EPSILON = 1e-06
@@ -395,6 +399,918 @@
     )
 
 
+BLOCK = 128
+TRUNK = 1024
+VMEM_BYTES = 62 * 1024 * 1024
+X_SWAP = [(0, 2), (2, 0), (1, 3), (3, 1)]
+CORE_SWAP = [(0, 1), (1, 0), (2, 3), (3, 2)]
+LOW = jnp.bfloat16
+F32 = jnp.float32
+
+
+def over_x(v):
+    return lax.ppermute(v, "context", X_SWAP)
+
+
+def over_core(v):
+    return lax.ppermute(v, "context", CORE_SWAP)
+
+
+def over_y(v):
+    return lax.ppermute(v, "tensor", [(0, 1), (1, 0)])
+
+
+def after(value, *others):
+    return lax.optimization_barrier((value,) + others)[0]
+
+
+def call(body, grid, ins, outs, flops, scratch=(), name=None):
+    in_specs, operands = [], []
+    for array, block, where in ins:
+        operands.append(array)
+        if block is None:
+            in_specs.append(pl.BlockSpec(memory_space=where))
+        elif where is None:
+            zero = (0,) * array.ndim
+            in_specs.append(
+                pl.BlockSpec(block, lambda *_, zero=zero: zero, pipeline_mode=pl.Buffered(1))
+            )
+        else:
+            in_specs.append(pl.BlockSpec(block, where))
+    out_specs, out_shape = [], []
+    for shape, kind, block, where in outs:
+        out_shape.append(jax.ShapeDtypeStruct(shape, kind))
+        if block is None:
+            out_specs.append(pl.BlockSpec(memory_space=where))
+        else:
+            out_specs.append(pl.BlockSpec(block, where))
+    moved = sum(a.size * a.dtype.itemsize for a in operands)
+    moved += sum(s.size * s.dtype.itemsize for s in out_shape)
+    return pl.pallas_call(
+        body,
+        grid=grid,
+        in_specs=in_specs,
+        out_specs=out_specs,
+        out_shape=out_shape,
+        scratch_shapes=list(scratch),
+        compiler_params=pltpu.CompilerParams(
+            vmem_limit_bytes=VMEM_BYTES, dimension_semantics=("arbitrary",) * len(grid)
+        ),
+        cost_estimate=pl.CostEstimate(flops=flops, bytes_accessed=moved, transcendentals=0),
+        name=name,
+    )(*operands)
+
+
+def mm(a, b):
+    return lax.dot_general(a, b, (((1,), (0,)), ((), ())), preferred_element_type=F32)
+
+
+def mm_t(a, b):
+    return lax.dot_general(a, b, (((1,), (1,)), ((), ())), preferred_element_type=F32)
+
+
+def prep_kernel(tok, gain, w_own, w_sis, w_gates, cos, sin, qg, kg, h_out, lin_own, lin_sis, pk_own, pk_sis):
+    t = tok[...].astype(F32)
+    h = (t * lax.rsqrt(jnp.mean(t * t, -1, keepdims=True) + EPSILON) * gain[...]).astype(LOW)
+    h_out[...] = h
+    logits = mm_t(h, w_gates[...])
+    high = logits.astype(LOW)
+    rest = (logits - high.astype(F32)).astype(LOW)
+    lane = lax.broadcasted_iota(jnp.int32, logits.shape, 1)
+    packed = jnp.where((lane & 2) == 0, high, rest)
+    c, s = cos[...], sin[...]
+    for w, lin, pk in ((w_own, lin_own, pk_own), (w_sis, lin_sis, pk_sis)):
+        u = mm(h, w[...])
+        lin[...] = u[:, : 3 * BLOCK]
+        for a in range(3):
+            head = u[:, a * BLOCK : (a + 1) * BLOCK]
+            g = (qg if a < 2 else kg)[...]
+            n = head * lax.rsqrt(jnp.mean(head * head, -1, keepdims=True) + EPSILON) * g
+            pk[:, a * BLOCK : (a + 1) * BLOCK] = (n * c + pltpu.roll(n, BLOCK // 2, 1) * s).astype(LOW)
+        pk[:, 3 * BLOCK : 4 * BLOCK] = u[:, 3 * BLOCK :].astype(LOW)
+        pk[:, 4 * BLOCK :] = packed
+
+
+def locate(tab, block):
+    return tab[0, block], pl.multiple_of(tab[1, block], BLOCK)
+
+
+def gate_column(buf, slot, row):
+    lanes = buf[slot, pl.ds(row, BLOCK), 4 * BLOCK :].astype(F32)
+    logits = []
+    for a in range(2):
+        own = lanes[:, a : a + 1] + lanes[:, a + 2 : a + 3]
+        sis = lanes[:, a + 4 : a + 5] + lanes[:, a + 6 : a + 7]
+        logits.append(jnp.where(slot == 0, own, sis))
+    return jax.nn.sigmoid(jnp.concatenate(logits, axis=0))
+
+
+def stack_heads(block):
+    return jnp.concatenate([block[:, :BLOCK], block[:, BLOCK:]], axis=0)
+
+
+def key_pieces(tab, i, pieces):
+    rows = 2 * BLOCK
+    out = []
+    for first, count in pieces:
+        slot, row = locate(tab, first)
+        limit = tab[2, i] - first * BLOCK
+
+        def keep(p, limit=limit, size=count * BLOCK):
+            col = lax.broadcasted_iota(jnp.int32, (rows, size), 1)
+            return jnp.where(col < limit, p, 0.0)
+
+        out.append((slot, row, count * BLOCK, keep))
+
+    def keep_parent(p):
+        return jnp.where(tab[5, i] > 0, p, 0.0)
+
+    def keep_own(p):
+        col = lax.broadcasted_iota(jnp.int32, (rows, BLOCK), 1)
+        row = lax.broadcasted_iota(jnp.int32, (rows, BLOCK), 0) & (BLOCK - 1)
+        return jnp.where(((col < row) & (tab[6, i] > 0)) | (col == row), p, 0.0)
+
+    out.append((tab[3, i], pl.multiple_of(tab[4, i], BLOCK), BLOCK, keep_parent))
+    slot, row = locate(tab, i)
+    out.append((slot, row, BLOCK, keep_own))
+    return out
+
+
+def attend_kernel(blocks, pieces, factor, tab, pk_own, pk_sis, out_own, out_sis, buf, held, sem):
+    copies = [
+        pltpu.make_async_copy(pk_own, buf.at[0], sem.at[0]),
+        pltpu.make_async_copy(pk_sis, buf.at[1], sem.at[1]),
+    ]
+    for cp in copies:
+        cp.start()
+    for cp in copies:
+        cp.wait()
+
+    def step(i, carry):
+        slot, row = locate(tab, i)
+        q = stack_heads(buf[slot, pl.ds(row, BLOCK), : 2 * BLOCK])
+        total = jnp.zeros((2 * BLOCK, 1), F32)
+        acc = jnp.zeros((2 * BLOCK, BLOCK), F32)
+        for ks, kr, size, keep in key_pieces(tab, i, pieces):
+            key = buf[ks, pl.ds(kr, size), 2 * BLOCK : 3 * BLOCK]
+            val = buf[ks, pl.ds(kr, size), 3 * BLOCK : 4 * BLOCK]
+            p = keep(jnp.exp2(mm_t(q, key) * factor))
+            total = total + jnp.sum(p, axis=-1, keepdims=True)
+            acc = acc + mm(p.astype(LOW), val)
+        gated = (acc * (gate_column(buf, slot, row) / total)).astype(LOW)
+        held[slot, pl.ds(row, BLOCK), :BLOCK] = gated[:BLOCK]
+        held[slot, pl.ds(row, BLOCK), BLOCK:] = gated[BLOCK:]
+        return carry
+
+    lax.fori_loop(0, blocks, step, 0)
+    copies = [
+        pltpu.make_async_copy(held.at[0], out_own, sem.at[0]),
+        pltpu.make_async_copy(held.at[1], out_sis, sem.at[1]),
+    ]
+    for cp in copies:
+        cp.start()
+    for cp in copies:
+        cp.wait()
+
+
+def attend_back_kernel(blocks, pieces, factor, scale, tab, *refs):
+    pk_own, pk_sis, ga_own, ga_sis, dg_own, dg_sis, out_own, out_sis, buf, ga, dg, held, dk, dv, sem = refs
+    copies = [
+        pltpu.make_async_copy(src, dst, sem.at[n])
+        for n, (src, dst) in enumerate(
+            [
+                (pk_own, buf.at[0]),
+                (pk_sis, buf.at[1]),
+                (ga_own, ga.at[0]),
+                (ga_sis, ga.at[1]),
+                (dg_own, dg.at[0]),
+                (dg_sis, dg.at[1]),
+            ]
+        )
+    ]
+    for cp in copies:
+        cp.start()
+    dk[...] = jnp.zeros_like(dk)
+    dv[...] = jnp.zeros_like(dv)
+    for cp in copies:
+        cp.wait()
+
+    def step(i, carry):
+        slot, row = locate(tab, i)
+        here = pl.ds(row, BLOCK)
+        q = stack_heads(buf[slot, here, : 2 * BLOCK])
+        gated = stack_heads(ga[slot, here, :]).astype(F32)
+        grad = stack_heads(dg[slot, here, :]).astype(F32)
+        gate = gate_column(buf, slot, row)
+        grad_gate = jnp.sum(grad * gated, axis=-1, keepdims=True) * (1.0 - gate)
+        grad_low = (grad * gate).astype(LOW)
+        q_t = q.astype(F32).T.astype(LOW)
+        grad_t = (grad * gate).T.astype(LOW)
+        runs = key_pieces(tab, i, pieces)
+        weights = []
+        total = jnp.zeros((2 * BLOCK, 1), F32)
+        for ks, kr, size, keep in runs:
+            key = buf[ks, pl.ds(kr, size), 2 * BLOCK : 3 * BLOCK]
+            p = keep(jnp.exp2(mm_t(q, key) * factor))
+            total = total + jnp.sum(p, axis=-1, keepdims=True)
+            weights.append(p)
+        inverse = 1.0 / total
+        delta = jnp.zeros((2 * BLOCK, 1), F32)
+        grad_probs = []
+        for (ks, kr, size, keep), p in zip(runs, weights):
+            val = buf[ks, pl.ds(kr, size), 3 * BLOCK : 4 * BLOCK]
+            grad_p = mm_t(grad_low, val)
+            delta = delta + jnp.sum(p * grad_p, axis=-1, keepdims=True)
+            grad_probs.append(grad_p)
+        delta = delta * inverse
+        grad_q = jnp.zeros((2 * BLOCK, BLOCK), F32)
+        for (ks, kr, size, keep), p, grad_p in zip(runs, weights, grad_probs):
+            key = buf[ks, pl.ds(kr, size), 2 * BLOCK : 3 * BLOCK]
+            probs = p * inverse
+            grad_s = (probs * (grad_p - delta)).astype(LOW)
+            grad_q = grad_q + mm(grad_s, key)
+            dk[ks, :, pl.ds(kr, size)] += mm(q_t, grad_s)
+            dv[ks, :, pl.ds(kr, size)] += mm(grad_t, probs.astype(LOW))
+        grad_q = (grad_q * scale).astype(LOW)
+        held[slot, here, :BLOCK] = grad_q[:BLOCK]
+        held[slot, here, BLOCK : 2 * BLOCK] = grad_q[BLOCK:]
+        lane = lax.broadcasted_iota(jnp.int32, (BLOCK, BLOCK), 1) - jnp.where(slot == 0, 0, 4)
+        lanes = jnp.where(lane == 0, grad_gate[:BLOCK], jnp.where(lane == 1, grad_gate[BLOCK:], 0.0))
+        held[slot, here, 4 * BLOCK :] = lanes.astype(LOW)
+        return carry
+
+    lax.fori_loop(0, blocks, step, 0)
+
+    def finish(i, carry):
+        slot, row = locate(tab, i)
+        here = pl.ds(row, BLOCK)
+        held[slot, here, 2 * BLOCK : 3 * BLOCK] = (dk[slot, :, here].T * scale).astype(LOW)
+        held[slot, here, 3 * BLOCK : 4 * BLOCK] = dv[slot, :, here].T.astype(LOW)
+        return carry
+
+    lax.fori_loop(0, blocks, finish, 0)
+    copies = [
+        pltpu.make_async_copy(held.at[0], out_own, sem.at[0]),
+        pltpu.make_async_copy(held.at[1], out_sis, sem.at[1]),
+    ]
+    for cp in copies:
+        cp.start()
+    for cp in copies:
+        cp.wait()
+
+
+def join_kernel(*refs):
+    pieces, weights = refs[:8], refs[8:16]
+    tok, gain, middle, hb = refs[16:]
+    acc = tok[...].astype(F32)
+    for g, w in zip(pieces, weights):
+        acc = acc + mm(g[...], w[...])
+
+    @pl.when(pl.program_id(0) == 0)
+    def _():
+        middle[...] = acc
+
+    hb[...] = (acc * lax.rsqrt(jnp.mean(acc * acc, -1, keepdims=True) + EPSILON) * gain[...]).astype(LOW)
+
+
+def units_kernel(hb, cot, w_gate, w_up, w_down, mixed, d_gate, d_up):
+    gate = mm(hb[...], w_gate[...])
+    up = mm(hb[...], w_up[...])
+    d_mixed = mm_t(cot[...], w_down[...])
+    sig = jax.nn.sigmoid(gate)
+    act = gate * sig
+    mixed[...] = (act * up).astype(LOW)
+    d_gate[...] = (d_mixed * up * sig * (1.0 + gate * (1.0 - sig))).astype(LOW)
+    d_up[...] = (d_mixed * act).astype(LOW)
+
+
+def spread(value, own, send_y, send_x, keep_a, keep_b):
+    step = pl.program_id(0)
+    half = value.shape[1] // 2
+    value = value.astype(LOW)
+
+    @pl.when(step == 0)
+    def _():
+        send_y[0] = value[:, :half]
+        send_x[0] = value[:, half:]
+
+    @pl.when(step == 1)
+    def _():
+        send_y[0] = value[:, :half]
+        keep_b[...] = value[:, half:]
+
+    @pl.when(step == 2)
+    def _():
+        keep_a[...] = value[:, :half]
+        send_x[0] = value[:, half:]
+
+    @pl.when(step == 3)
+    def _():
+        own[...] = value
+
+
+def step_block(s):
+    return jnp.where(s == 0, 3, jnp.where(s == 3, 0, s))
+
+
+def spread_outs(rows, width):
+    half = width // 2
+    return [
+        ((rows, width), LOW, (rows, width), lambda s: (0, 0)),
+        ((2, rows, half), LOW, (1, rows, half), lambda s: (jnp.where(s == 0, 1, 0), 0, 0)),
+        ((2, rows, half), LOW, (1, rows, half), lambda s: (jnp.where(s <= 1, 1, 0), 0, 0)),
+        ((rows, half), LOW, (rows, half), lambda s: (0, 0)),
+        ((rows, half), LOW, (rows, half), lambda s: (0, 0)),
+    ]
+
+
+def grad_hb_kernel(*refs):
+    grads, weights, (hb, own, send_y, send_x, keep_a, keep_b, total) = refs[:4], refs[4:8], refs[8:]
+    acc = mm_t(grads[0][...], weights[0][...])
+    for g, w in zip(grads[1:], weights[1:]):
+        acc = acc + mm_t(g[...], w[...])
+
+    @pl.when(pl.program_id(0) == 0)
+    def _():
+        total[...] = jnp.zeros_like(total)
+
+    total[...] += jnp.sum(acc * hb[...].astype(F32), axis=0, keepdims=True)
+    spread(acc, own, send_y, send_x, keep_a, keep_b)
+
+
+def down_kernel(m_own, m_sis, w_own, w_sis, own, send_y, send_x, keep_a, keep_b):
+    spread(mm(m_own[...], w_own[...]) + mm(m_sis[...], w_sis[...]), own, send_y, send_x, keep_a, keep_b)
+
+
+def gathered(own, from_y, from_x, last_a, last_b):
+    half = own.shape[1] // 2
+    left = own[:, :half].astype(F32) + from_y[0].astype(F32) + last_a[...].astype(F32)
+    right = own[:, half:].astype(F32) + from_x[0].astype(F32) + last_b[...].astype(F32)
+    return jnp.concatenate([left, right], axis=1)
+
+
+def norm_back(value, gain, incoming):
+    r = lax.rsqrt(jnp.mean(value * value, -1, keepdims=True) + EPSILON)
+    hat = value * r
+    t = incoming * gain
+    return r * (t - hat * jnp.mean(t * hat, -1, keepdims=True))
+
+
+def turn_kernel(own, from_y, from_x, last_a, last_b, middle, cot, gain, *refs):
+    weights, (d_middle, attn_a, attn_b, g_own, g_y, g_yd, g_x, g_xd) = refs[:8], refs[8:]
+    incoming = gathered(own[...], from_y, from_x, last_a, last_b)
+    grad = cot[...].astype(F32) + norm_back(middle[...], gain[...], incoming)
+    d_middle[...] = grad
+    low = grad.astype(LOW)
+    half = low.shape[1] // 2
+    attn_a[...] = low[:, :half]
+    attn_b[...] = low[:, half:]
+    width = weights[0].shape[0]
+    for n, (ref, at) in enumerate(
+        [(g_own, 0), (g_own, 1), (g_y, 0), (g_y, 1), (g_x, 0), (g_x, 1), (g_xd, 0), (g_yd, 0)]
+    ):
+        ref[:, at * width : (at + 1) * width] = mm_t(low, weights[n][...]).astype(LOW)
+
+
+def heads_back_kernel(
+    dp_own, dp_sis, lin_own, lin_sis, h, w_own, w_sis, w_gates, cos, sin, qg, kg,
+    own, send_y, send_x, keep_a, keep_b, dl_own, dl_sis, dl_gate, q_sum, k_sum, total,
+):
+    step = pl.program_id(0)
+
+    @pl.when(step == 0)
+    def _():
+        q_sum[...] = jnp.zeros_like(q_sum)
+        k_sum[...] = jnp.zeros_like(k_sum)
+        total[...] = jnp.zeros_like(total)
+
+    c, s = cos[...], sin[...]
+    for dp, lin, dl in ((dp_own, lin_own, dl_own), (dp_sis, lin_sis, dl_sis)):
+        for a in range(3):
+            at = slice(a * BLOCK, (a + 1) * BLOCK)
+            w = dp[:, at].astype(F32)
+            n = w * c - pltpu.roll(w, BLOCK // 2, 1) * s
+            u = lin[:, at]
+            r = lax.rsqrt(jnp.mean(u * u, -1, keepdims=True) + EPSILON)
+            hat = u * r
+            into = q_sum if a < 2 else k_sum
+            into[...] += jnp.sum(n * hat, axis=0, keepdims=True)
+            t = n * (qg if a < 2 else kg)[...]
+            dl[:, at] = (r * (t - hat * jnp.mean(t * hat, -1, keepdims=True))).astype(LOW)
+        dl[:, 3 * BLOCK :] = dp[:, 3 * BLOCK : 4 * BLOCK]
+    gates = dp_own[:, 4 * BLOCK :] + dp_sis[:, 4 * BLOCK :]
+    dl_gate[...] = gates
+    acc = mm_t(dl_own[...], w_own[...]) + mm_t(dl_sis[...], w_sis[...]) + mm(gates, w_gates[...])
+    total[...] += jnp.sum(acc * h[...].astype(F32), axis=0, keepdims=True)
+    spread(acc, own, send_y, send_x, keep_a, keep_b)
+
+
+def last_kernel(own, from_y, from_x, last_a, last_b, tok, gain, d_middle, out, out_low):
+    incoming = gathered(own[...], from_y, from_x, last_a, last_b)
+    grad = d_middle[...] + norm_back(tok[...].astype(F32), gain[...], incoming)
+    low = grad.astype(LOW)
+    out_low[...] = low
+    out[...] = low.astype(F32)
+
+
+def place_kernel(axis, parts, idx, *refs):
+    blocks, outs = refs[:4], refs[4:]
+    turn = jnp.bitwise_xor(pl.program_id(0), idx[0])
+    for n in range(4):
+
+        @pl.when(turn == n)
+        def _(n=n):
+            for (lo, hi), out in zip(parts, outs):
+                out[...] = blocks[n][:, lo:hi].astype(F32) if axis else blocks[n][...].astype(F32)
+
+
+def line_gather(piece, z, axis, first=None):
+    right = [(0, 1), (1, 2), (2, 3)]
+    left = [(1, 0), (2, 1), (3, 2)]
+    if first is not None:
+        piece = after(piece, *first)
+    r1 = lax.ppermute(piece, "wide", right)
+    l1 = lax.ppermute(piece, "wide", left)
+    r2 = lax.ppermute(r1, "wide", right[1:])
+    l2 = lax.ppermute(l1, "wide", left[:2])
+    r3 = lax.ppermute(r2, "wide", right[2:])
+    l3 = lax.ppermute(l2, "wide", left[:1])
+    s1 = jnp.where(z >= 1, r1, l3)
+    s2 = jnp.where(z >= 2, r2, l2)
+    s3 = jnp.where(z == 3, r3, l1)
+    size = piece.shape[axis]
+    shape = list(piece.shape)
+    shape[axis] = 4 * size
+    full = jnp.zeros(shape, piece.dtype)
+    for k, part in enumerate((piece, s3, s2, s1)):
+        full = lax.dynamic_update_slice_in_dim(full, part, ((z + k) % 4) * size, axis)
+    return full, (r1, l1)
+
+
+def line_scatter(whole, z, axis):
+    size = whole.shape[axis] // 4
+    right = [(0, 1), (1, 2), (2, 3)]
+    left = [(1, 0), (2, 1), (3, 2)]
+
+    def part(offset):
+        return lax.dynamic_slice_in_dim(whole, ((z + offset + 4) % 4) * size, size, axis)
+
+    def plus(a, b):
+        return (a.astype(F32) + b.astype(F32)).astype(LOW)
+
+    a = lax.ppermute(part(3), "wide", right[:1])
+    b = lax.ppermute(part(-3), "wide", left[2:])
+    a = lax.ppermute(plus(part(2), a), "wide", right[:2])
+    b = lax.ppermute(plus(part(-2), b), "wide", left[1:])
+    a = lax.ppermute(plus(part(1), a), "wide", right)
+    b = lax.ppermute(plus(part(-1), b), "wide", left)
+    return (part(0).astype(F32) + a.astype(F32) + b.astype(F32)).astype(LOW)
+
+
+def four(a, b):
+    x_a, y_b = over_x(a), over_y(b)
+    y_a, x_b = over_y(a), over_x(b)
+    d_a, d_b = over_y(x_a), over_x(y_b)
+    return [(a, b), (y_a, y_b), (x_a, x_b), (d_a, d_b)]
+
+
+def plane_sum(own, send_y, send_x, keep_a, keep_b):
+    from_y = over_y(send_y)
+    from_x = over_x(send_x)
+    last_a = over_x((keep_a.astype(F32) + from_y[1].astype(F32)).astype(LOW))
+    last_b = over_y((keep_b.astype(F32) + from_x[1].astype(F32)).astype(LOW))
+    return own, from_y, from_x, last_a, last_b
+
+
+def plane_ins(pieces):
+    own, from_y, from_x, last_a, last_b = pieces
+    rows, width = own.shape
+    half = width // 2
+    return [
+        (own, (rows, width), lambda s: (0, 0)),
+        (from_y, (1, rows, half), lambda s: (0, 0, 0)),
+        (from_x, (1, rows, half), lambda s: (0, 0, 0)),
+        (last_a, (rows, half), lambda s: (0, 0)),
+        (last_b, (rows, half), lambda s: (0, 0)),
+    ]
+
+
+def place(shard, idx, axis, parts):
+    from_core, from_x = over_core(shard), over_x(shard)
+    blocks = [shard, from_core, from_x, over_core(from_x)]
+    rows, width = shard.shape
+    outs = []
+    for lo, hi in parts:
+        if axis:
+            outs.append(((rows, 4 * (hi - lo)), F32, (rows, hi - lo), lambda p: (0, p)))
+        else:
+            outs.append(((4 * rows, width), F32, (rows, width), lambda p: (p, 0)))
+    return call(
+        functools.partial(place_kernel, axis, parts),
+        (4,),
+        [(idx, None, pltpu.SMEM)] + [(b, (rows, width), None) for b in blocks],
+        outs,
+        0,
+        name="place",
+    )
+
+
+def total_over(values, axes):
+    for move in axes:
+        values = values + move(values)
+    return values
+
+
+def visit_table(segment_of, parent_of, valid, x, core, y, rows):
+    per = rows // BLOCK
+    half = per // 2
+    i = jnp.arange(4 * per, dtype=jnp.int32)
+    seg, live = segment_of[::BLOCK], valid[::BLOCK]
+    context = i // per
+    slot = (context % 2) ^ core
+    block = ((context // 2) ^ x) * 2 + ((i % per) // half ^ y)
+    row = (block * half + i % half) * BLOCK
+    trunk = seg[0]
+    parent = jnp.sum(
+        jnp.where(seg[:, None] == jnp.arange(parent_of.shape[0])[None, :], parent_of[None, :], 0), axis=1
+    )
+    has = (live > 0) & (seg != trunk) & (parent != trunk)
+    match = (live[None, :] > 0) & (seg[None, :] == parent[:, None])
+    where = jnp.min(jnp.where(match, i[None, :], 4 * per - 1), axis=1)
+    pick = where[:, None] == i[None, :]
+    p_slot = jnp.sum(jnp.where(pick, slot[None, :], 0), axis=1)
+    p_row = jnp.sum(jnp.where(pick, row[None, :], 0), axis=1)
+    limit = jnp.where(live > 0, jnp.where(seg == trunk, i * BLOCK, TRUNK), 0)
+    return jnp.stack([slot, row, limit, p_slot, p_row, has.astype(jnp.int32), live]).astype(jnp.int32)
+
+
+def plane_shards(
+    tokens, segment_of, parent_of, valid, positions, g_attn, w_q, key_projection, value_projection, w_g,
+    q_gain, k_gain, w_o, g_mlp, w_gate, w_up, w_down, cotangent,
+):
+    rows, width = tokens.shape
+    part = rows // 2
+    z, c, y = lax.axis_index("wide"), lax.axis_index("context"), lax.axis_index("tensor")
+    x, core = c // 2, c % 2
+    scale = BLOCK ** (-0.5)
+    factor = scale * 1.4426950408889634
+
+    def cut(w, axis):
+        size = w.shape[axis] // 4
+        return lax.dynamic_slice_in_dim(w, c * size, size, axis)
+
+    depth = w_q.shape[0]
+    small = jnp.concatenate(
+        [g_attn[None, :], g_mlp[None, :], w_g.T, jnp.zeros((6, depth), LOW)], axis=0
+    )
+    small_full, small_step = line_gather(small, z, 1)
+    attn_gain = small_full[0:1].astype(F32)
+    mlp_gain = small_full[1:2].astype(F32)
+    gates_t = small_full[2:10]
+    own_rows = lax.dynamic_slice_in_dim(gates_t, 2 * c, 2, 0)
+    sis_rows = lax.dynamic_slice_in_dim(gates_t, 2 * (c ^ 1), 2, 0)
+    gate_rows = jnp.concatenate(
+        [own_rows, own_rows, sis_rows, sis_rows, jnp.zeros((BLOCK - 8, width), LOW)], axis=0
+    )
+
+    qkv = jnp.concatenate([cut(w_q, 1), cut(key_projection, 1), cut(value_projection, 1)], axis=1)
+    qkv_own, st = line_gather(qkv, z, 0)
+    wo_own, st = line_gather(cut(w_o, 0), z, 1, st)
+    wg_own, st = line_gather(cut(w_gate, 1), z, 0, st)
+    wu_own, st = line_gather(cut(w_up, 1), z, 0, st)
+    wd_own, st = line_gather(cut(w_down, 0), z, 1, st)
+    qkv_sis = over_core(qkv_own)
+    wo_sis = over_core(wo_own)
+    wg_sis, wu_sis, wd_sis = over_core(wg_own), over_core(wu_own), over_core(wd_own)
+
+    def halves(v):
+        return (
+            lax.dynamic_slice_in_dim(v, y * part, part, 0),
+            lax.dynamic_slice_in_dim(v, (1 - y) * part, part, 0),
+        )
+
+    tok0, tok1 = halves(tokens)
+    cut2 = part // 2
+    t2 = [over_x(tok0[:cut2]), over_x(tok0[cut2:])]
+    t3 = [over_y(v) for v in t2]
+    tok_near = jnp.concatenate([tok0, tok1], axis=0)
+    tok_far = jnp.concatenate(t2 + t3, axis=0)
+    cot0, cot1 = halves(cotangent)
+    cot_first = after(cot0, *t3)
+    c2 = [over_x(cot_first[:cut2]), over_x(cot_first[cut2:])]
+    c3 = [over_y(v) for v in c2]
+    cot = jnp.concatenate([cot0, cot1] + c2 + c3, axis=0)
+
+    pos = positions.astype(F32).reshape(rows // BLOCK, BLOCK)
+    pos_far = over_x(pos)
+
+    def tables(p):
+        p0, p1 = halves(p.reshape(rows))
+        cosine, sine = rope_tables(jnp.concatenate([p0, p1]), BLOCK)
+        sign = jnp.where(jnp.arange(BLOCK) < BLOCK // 2, -1.0, 1.0)
+        return cosine, sine * sign
+
+    qg, kg = q_gain.astype(F32)[None, :], k_gain.astype(F32)[None, :]
+    near_tables, far_tables = tables(pos), tables(pos_far)
+    three, four_, five = 3 * BLOCK, 4 * BLOCK, 5 * BLOCK
+
+    def prep(tok, tab):
+        return call(
+            prep_kernel,
+            (2,),
+            [
+                (tok, (part, width), lambda s: (s, 0)),
+                (attn_gain, (1, width), None),
+                (qkv_own, qkv_own.shape, None),
+                (qkv_sis, qkv_sis.shape, None),
+                (gate_rows, gate_rows.shape, None),
+                (tab[0], (part, BLOCK), lambda s: (s, 0)),
+                (tab[1], (part, BLOCK), lambda s: (s, 0)),
+                (qg, (1, BLOCK), None),
+                (kg, (1, BLOCK), None),
+            ],
+            [
+                ((rows, width), LOW, (part, width), lambda s: (s, 0)),
+                ((rows, three), F32, (part, three), lambda s: (s, 0)),
+                ((rows, three), F32, (part, three), lambda s: (s, 0)),
+                ((rows, five), LOW, (part, five), lambda s: (s, 0)),
+                ((rows, five), LOW, (part, five), lambda s: (s, 0)),
+            ],
+            2 * rows * width * 9 * BLOCK,
+            name="prep",
+        )
+
+    near = prep(tok_near, near_tables)
+    far = prep(tok_far, far_tables)
+    pk_own = jnp.concatenate([near[3], far[3]], axis=0)
+    pk_sis = jnp.concatenate([over_core(near[4]), over_core(far[4])], axis=0)
+
+    tab = visit_table(segment_of, parent_of, valid, x, core, y, rows)
+    per = rows // BLOCK
+    half = per // 2
+    blocks = 4 * per
+    pieces = [(f, min(half, TRUNK // BLOCK - f)) for f in range(0, TRUNK // BLOCK, half)]
+    all_rows = 2 * rows
+    ANY, SMEM, VMEM = pl.ANY, pltpu.SMEM, pltpu.VMEM
+    gated_own, gated_out = call(
+        functools.partial(attend_kernel, blocks, pieces, factor),
+        (1,),
+        [(tab, None, SMEM), (pk_own, None, ANY), (pk_sis, None, ANY)],
+        [((all_rows, 2 * BLOCK), LOW, None, ANY)] * 2,
+        blocks * 4 * 256 * 1280 * 128,
+        scratch=[
+            VMEM((2, all_rows, five), LOW),
+            VMEM((2, all_rows, 2 * BLOCK), LOW),
+            pltpu.SemaphoreType.DMA((2,)),
+        ],
+        name="attend",
+    )
+    gated_sis = over_core(gated_out)
+    gated = four(gated_own, gated_sis)
+    wo = four(wo_own, wo_sis)
+    tok_all = jnp.concatenate([tok_near, tok_far], axis=0)
+    two = 2 * BLOCK
+    turns = [0, 1, 2, 3]
+    middle, hb = call(
+        join_kernel,
+        (4,),
+        [(g, (part, two), lambda s, t=t: (s ^ t, 0)) for t, pair in zip(turns, gated) for g in pair]
+        + [(w, (two, width), None) for pair in wo for w in pair]
+        + [(tok_all, (part, width), lambda s: (s, 0)), (mlp_gain, (1, width), None)],
+        [
+            ((part, width), F32, (part, width), lambda s: (0, 0)),
+            ((all_rows, width), LOW, (part, width), lambda s: (s, 0)),
+        ],
+        2 * all_rows * width * width,
+        name="join",
+    )
+
+    units = wg_own.shape[1]
+
+    def hidden(wg, wu, wd):
+        return call(
+            units_kernel,
+            (4,),
+            [
+                (hb, (part, width), lambda s: (s, 0)),
+                (cot, (part, width), lambda s: (s, 0)),
+                (wg, wg.shape, None),
+                (wu, wu.shape, None),
+                (wd, wd.shape, None),
+            ],
+            [((all_rows, units), LOW, (part, units), lambda s: (s, 0))] * 3,
+            6 * all_rows * width * units,
+            name="units",
+        )
+
+    mixed_own, dg_own, du_own = hidden(wg_own, wu_own, wd_own)
+    mixed_sis, dg_sis, du_sis = hidden(wg_sis, wu_sis, wd_sis)
+
+    by_block = lambda s: (step_block(s), 0)
+    total_spec = ((1, width), F32, (1, width), lambda s: (0, 0))
+    *dhb, hb_total = call(
+        grad_hb_kernel,
+        (4,),
+        [(g, (part, units), by_block) for g in (dg_own, du_own, dg_sis, du_sis)]
+        + [(w, w.shape, None) for w in (wg_own, wu_own, wg_sis, wu_sis)]
+        + [(hb, (part, width), by_block)],
+        spread_outs(part, width) + [total_spec],
+        8 * all_rows * width * units,
+        name="grad_hb",
+    )
+    dhb = plane_sum(*dhb)
+
+    out_parts = call(
+        down_kernel,
+        (4,),
+        [
+            (mixed_own, (part, units), by_block),
+            (mixed_sis, (part, units), by_block),
+            (wd_own, wd_own.shape, None),
+            (wd_sis, wd_sis.shape, None),
+        ],
+        spread_outs(part, width),
+        4 * all_rows * width * units,
+        name="down",
+    )
+
+    def core_sum(sent, kept):
+        return (kept + over_core(sent.astype(LOW)).astype(F32)).astype(LOW)
+
+    gd = core_sum(product_left(mixed_sis, cot), product_left(mixed_own, cot))
+    gg = core_sum(product_left(hb, dg_sis), product_left(hb, dg_own))
+    gu = core_sum(product_left(hb, du_sis), product_left(hb, du_own))
+    gd_shard = line_scatter(gd, z, 1)
+    gg_shard = line_scatter(gg, z, 0)
+    gu_shard = line_scatter(gu, z, 0)
+
+    flat = [(w, w.shape, None) for pair in wo for w in pair]
+    half_w = width // 2
+    first = lambda s: (0, 0)
+    d_middle, attn_a, attn_b, g_own, g_y, g_yd, g_x, g_xd = call(
+        turn_kernel,
+        (1,),
+        plane_ins(dhb)
+        + [
+            (middle, (part, width), first),
+            (cot, (part, width), first),
+            (mlp_gain, (1, width), first),
+        ]
+        + flat,
+        [
+            ((part, width), F32, (part, width), first),
+            ((part, half_w), LOW, (part, half_w), first),
+            ((part, half_w), LOW, (part, half_w), first),
+            ((part, 2 * two), LOW, (part, 2 * two), first),
+            ((part, 2 * two), LOW, (part, 2 * two), first),
+            ((part, two), LOW, (part, two), first),
+            ((part, 2 * two), LOW, (part, 2 * two), first),
+            ((part, two), LOW, (part, two), first),
+        ],
+        2 * part * width * width,
+        name="turn",
+    )
+    r_y, r_x = over_y(g_y), over_x(g_x)
+    r_xd, r_yd = over_y(over_x(g_xd)), over_x(over_y(g_yd))
+    dgated_own = jnp.concatenate([g_own[:, :two], r_y[:, :two], r_x[:, :two], r_xd], axis=0)
+    dgated_sis = over_core(jnp.concatenate([g_own[:, two:], r_y[:, two:], r_x[:, two:], r_yd], axis=0))
+    dp_own, dp_out = call(
+        functools.partial(attend_back_kernel, blocks, pieces, factor, scale),
+        (1,),
+        [(tab, None, SMEM)]
+        + [(v, None, ANY) for v in (pk_own, pk_sis, gated_own, gated_out, dgated_own, dgated_sis)],
+        [((all_rows, five), LOW, None, ANY)] * 2,
+        blocks * 10 * 256 * 1280 * 128,
+        scratch=[
+            VMEM((2, all_rows, five), LOW),
+            VMEM((2, all_rows, two), LOW),
+            VMEM((2, all_rows, two), LOW),
+            VMEM((2, all_rows, five), LOW),
+            VMEM((2, BLOCK, all_rows), F32),
+            VMEM((2, BLOCK, all_rows), F32),
+            pltpu.SemaphoreType.DMA((6,)),
+        ],
+        name="attend_back",
+    )
+    dp_sis = over_core(dp_out)
+    lin_own = jnp.concatenate([near[1], far[1]], axis=0)
+    lin_sis = jnp.concatenate([near[2], far[2]], axis=0)
+    h = jnp.concatenate([near[0], far[0]], axis=0)
+    cos = jnp.concatenate([near_tables[0], far_tables[0]], axis=0)
+    sin = jnp.concatenate([near_tables[1], far_tables[1]], axis=0)
+    one = ((1, BLOCK), F32, (1, BLOCK), first)
+    *dh, dl_own, dl_sis, dl_gate, q_sum, k_sum, h_total = call(
+        heads_back_kernel,
+        (4,),
+        [
+            (dp_own, (part, five), by_block),
+            (dp_sis, (part, five), by_block),
+            (lin_own, (part, three), by_block),
+            (lin_sis, (part, three), by_block),
+            (h, (part, width), by_block),
+            (qkv_own, qkv_own.shape, None),
+            (qkv_sis, qkv_sis.shape, None),
+            (gate_rows, gate_rows.shape, None),
+            (cos, (part, BLOCK), by_block),
+            (sin, (part, BLOCK), by_block),
+            (qg, (1, BLOCK), None),
+            (kg, (1, BLOCK), None),
+        ],
+        spread_outs(part, width)
+        + [
+            ((all_rows, four_), LOW, (part, four_), by_block),
+            ((all_rows, four_), LOW, (part, four_), by_block),
+            ((all_rows, BLOCK), LOW, (part, BLOCK), by_block),
+            one,
+            one,
+            total_spec,
+        ],
+        2 * all_rows * width * 9 * BLOCK,
+        name="heads_back",
+    )
+    dh = plane_sum(*dh)
+    grad_tokens_own, grad_low = call(
+        last_kernel,
+        (1,),
+        plane_ins(dh)
+        + [
+            (tok0, (part, width), first),
+            (attn_gain, (1, width), first),
+            (d_middle, (part, width), first),
+        ],
+        [((part, width), F32, (part, width), first), ((part, width), LOW, (part, width), first)],
+        part * width * 16,
+        name="last",
+    )
+
+    def both_halves(mine, other):
+        return jnp.where(
+            y == 0, jnp.concatenate([mine, other], axis=0), jnp.concatenate([other, mine], axis=0)
+        )
+
+    grad_tokens = both_halves(grad_tokens_own, over_y(grad_low).astype(F32))
+
+    gq = core_sum(product_left(h, dl_sis), product_left(h, dl_own))
+    gq_shard = line_scatter(gq, z, 0)
+    attn_low = four(attn_a, attn_b)
+    order = [attn_low[0], attn_low[1], attn_low[2], attn_low[3]]
+    d_attn = jnp.concatenate(
+        [jnp.concatenate([a for a, _ in order], axis=0), jnp.concatenate([b for _, b in order], axis=0)], axis=1
+    )
+    go = core_sum(product_left(gated_sis, d_attn), product_left(gated_own, d_attn))
+    go_shard = line_scatter(go, z, 1)
+
+    sums = plane_sum(*out_parts)
+    out_own = (middle + gathered(*sums)).astype(LOW)
+    layer_out = both_halves(out_own, over_y(out_own))
+
+    gate_grad = product_left(dl_gate, h)
+    rows_of = jnp.arange(8, dtype=jnp.int32)[:, None]
+    gate_rows_grad = jnp.zeros((8, width), F32)
+    for n, row in ((0, 2 * c), (1, 2 * c + 1), (4, 2 * (c ^ 1)), (5, 2 * (c ^ 1) + 1)):
+        gate_rows_grad = gate_rows_grad + jnp.where(rows_of == row, gate_grad[n : n + 1], 0.0)
+    gains = jnp.concatenate(
+        [
+            h_total / attn_gain,
+            hb_total / mlp_gain,
+            jnp.concatenate([q_sum, k_sum, jnp.zeros((1, width - two), F32)], axis=1),
+            jnp.zeros((5, width), F32),
+        ],
+        axis=0,
+    )
+    gains = gains + over_y(gains)
+    packed = jnp.concatenate([gate_rows_grad, gains], axis=0)
+    packed = packed + over_core(packed)
+    packed = packed + over_x(packed)
+    packed = packed + lax.ppermute(packed, "wide", [(0, 1), (1, 0), (2, 3), (3, 2)])
+    packed = packed + lax.ppermute(packed, "wide", [(0, 2), (2, 0), (1, 3), (3, 1)])
+    mine = lax.dynamic_slice_in_dim(packed, z * depth, depth, 1)
+
+    idx = c.reshape(1).astype(jnp.int32)
+    whole_units = [(0, units)]
+    (final_gate,) = place(gg_shard, idx, 1, whole_units)
+    (final_up,) = place(gu_shard, idx, 1, whole_units)
+    (final_down,) = place(gd_shard, idx, 0, [(0, depth)])
+    (final_out,) = place(go_shard, idx, 0, [(0, depth)])
+    final_q, final_k, final_v = place(gq_shard, idx, 1, [(0, two), (two, three), (three, four_)])
+    return (
+        layer_out,
+        grad_tokens,
+        mine[8],
+        final_q,
+        final_k,
+        final_v,
+        mine[:8].T,
+        packed[10, :BLOCK],
+        packed[10, BLOCK:two],
+        final_out,
+        mine[9],
+        final_gate,
+        final_up,
+        final_down,
+    )
+
+
 def solution(mesh):
     placed = (
         P(("wide", "context"), None),
@@ -416,8 +1332,9 @@
         P("tensor", "wide"),
         P(("wide", "context"), None),
     )
+    in_planes = mesh.shape["wide"] == 4 and mesh.shape["context"] == 4 and mesh.shape["tensor"] == 2
     return jax.shard_map(
-        shards,
+        plane_shards if in_planes else shards,
         mesh=mesh,
         in_specs=placed,
         out_specs=(

time: 3130 us -> 1090 us (0.35)
  waiting for transfers between devices: 2220 us -> 329 us
  matrix products: 463 us -> 74.9 us
  Pallas kernels: 0 us -> 269 us
  starting transfers between devices: 1.23 us -> 216 us
  local copies, waits for them, and re-layouts: 174 us -> 74.7 us
  blocking collectives: 84.7 us -> 0 us
  other arithmetic: 159 us -> 112 us
    reduce_scatter x12 -> x0, waiting for transfers between devices: 969 us -> none  [the longest x1 215 us: shards(): lax.psum_scatter(grad_up_w.astype(jnp.bfloat16), 'wide', scatter_dimensio...]
    all_gather x11 -> x0, waiting for transfers between devices: 799 us -> none  [the longest x1 210 us: shards(): lax.all_gather(w_gate, 'wide', axis=0, tiled=True)]
    psum x3 -> x0, waiting for transfers between devices: 447 us -> none  [the longest x1 220 us: shards(): lax.psum(share_query.astype(jnp.bfloat16), 'context').astype(jnp.float32)]
    dot_general x125 -> x0, matrix products: 391 us -> none  [the longest x32 113 us: product_right(): lax.dot_general(left, right, (((1,), (1,)), ((), ())), preferred_element_...]
    ppermute x0 -> x148, waiting for transfers between devices: none -> 329 us  [the longest x29 108 us: over_x(): return lax.ppermute(v, 'context', X_SWAP)]
    pallas_call x0 -> x17, Pallas kernels: none -> 269 us  [call(): pl.pallas_call(body, grid=grid, in_specs=in_specs, out_specs=out_specs, o...]
    ppermute x0 -> x148, starting transfers between devices: none -> 216 us  [the longest x5 32.7 us: line_scatter(): a = lax.ppermute(plus(part(1), a), 'wide', right)]
    reduce_sum x22 -> x2, other arithmetic: 48.1 us -> 0.27 us  [the longest x1 0.18 us: visit_table(): p_row = jnp.sum(jnp.where(pick, row[None, :], 0), axis=1)]
  transfers between devices with their start and end apart: 26 -> 148, of which waited for: 22 -> 46; matrix products, arithmetic and copies ran while one was open for 12% -> 23% of each run, Pallas kernels for 0% -> 21%
where the time goes in v1:
time: 1090 us; the launch traced here: 1080 us
  waiting for transfers between devices  329 us (30%)
  Pallas kernels  269 us (25%)
  starting transfers between devices  216 us (20%)
  other arithmetic  112 us (10%)
  matrix products  74.9 us (7%)
  local copies, waits for them, and re-layouts  74.7 us (7%)
    pallas_call x17, Pallas kernels, call(): pl.pallas_call(body, grid=grid, in_specs=in_specs, out_specs=out_specs, o...  269 us
    ppermute x29, waiting for transfers between devices, over_x(): return lax.ppermute(v, 'context', X_SWAP)  108 us
    dot_general x11, matrix products, product_left(): lax.dot_general(left, right, (((0,), (0,)), ((), ())), preferred_element_...  74.9 us
    ppermute x25, waiting for transfers between devices, over_y(): return lax.ppermute(v, 'tensor', [(0, 1), (1, 0)])  50.2 us
    ppermute x6, waiting for transfers between devices, line_gather(): l3 = lax.ppermute(l2, 'wide', left[:1])  50.2 us
    unnamed x243, local copies, waits for them, and re-layouts  33.8 us
    ppermute x5, starting transfers between devices, line_scatter(): a = lax.ppermute(plus(part(1), a), 'wide', right)  32.7 us
    ppermute x29, starting transfers between devices, over_x(): return lax.ppermute(v, 'context', X_SWAP)  31.7 us
  transfers between devices with their start and end apart: 148, of which 46 were waited for; matrix products, arithmetic and copies ran while one was open for 23% of the time, Pallas kernels for 21%

profile of v1, /device:TPU:0, one launch (start us, length us, event | category | flops | bytes accessed | tf_op | source)
XLA Modules:
  0.0 1079.0 jit_solution(13912869983687687456)
XLA Ops:
  111.3 17.7 %collective-permute-done.32 = bf16[256,512]{1,0:T(8,128)(2,1)S(1)} collective-permute-done((bf16[256,512]{1,0:T(8,128)(2,1)S(1)}, bf16[256,512]{1,0:T(8,128)(2,1)S(1)}, u32[]{:S(2)}, u32[]{:S(2)}) %collective-permute-start.32) | collective-permute-done | bytes 262176 | tf_op jit(solution)/shard_map/ppermute | solution.py:837
  171.0 11.4 %collective-permute-done.48 = bf16[512,768]{1,0:T(8,128)(2,1)S(1)} collective-permute-done((bf16[512,768]{1,0:T(8,128)(2,1)S(1)}, bf16[512,768]{1,0:T(8,128)(2,1)S(1)}, u32[]{:S(2)}, u32[]{:S(2)}) %collective-permute-start.48) | collective-permute-done | bytes 786464 | tf_op jit(solution)/shard_map/ppermute | solution.py:835
  211.3 10.1 prep.2
  226.9 10.2 prep.3
  269.3 24.2 %attend.1 = (bf16[1536,256]{1,0:T(8,128)(2,1)}, bf16[1536,256]{1,0:T(8,128)(2,1)}) custom-call(s32[7,24]{1,0:T(8,128)} %stack.26.tab, bf16[1536,640]{1,0:T(8,128)(2,1)} %copy-done.68, bf16[1536,640]{1,0:T(8,128)(2,1)} %copy-done.69), custom_call_target="tpu_custom_call" | custom-call | flops 4026531840 | bytes 5505696 | tf_op jit(solution)/shard_map/attend/pallas_call | solution.py:449
  320.8 10.1 collective-permute-done.61
  337.0 10.6 collective-permute-done.23.refs_4_
  351.0 13.4 %collective-permute-done.24.refs_5_ = bf16[1536,256]{1,0:T(8,128)(2,1)S(1)} collective-permute-done((bf16[1536,256]{1,0:T(8,128)(2,1)S(1)}, bf16[1536,256]{1,0:T(8,128)(2,1)S(1)}, u32[]{:S(2)}, u32[]{:S(2)}) %collective-permute-start.24) | collective-permute-done | bytes 786464 | tf_op jit(solution)/shard_map/ppermute | solution.py:412
  369.0 11.9 %collective-permute-done.26.refs_7_ = bf16[1536,256]{1,0:T(8,128)(2,1)S(1)} collective-permute-done((bf16[1536,256]{1,0:T(8,128)(2,1)S(1)}, bf16[1536,256]{1,0:T(8,128)(2,1)S(1)}, u32[]{:S(2)}, u32[]{:S(2)}) %collective-permute-start.26) | collective-permute-done | bytes 786464 | tf_op jit(solution)/shard_map/ppermute | solution.py:412
  381.8 22.9 %join.1 = (f32[384,2048]{1,0:T(8,128)}, bf16[1536,2048]{1,0:T(8,128)(2,1)}) custom-call(bf16[1536,256]{1,0:T(8,128)(2,1)} %get-tuple-element.80.refs_0_.refs_2_, bf16[1536,256]{1,0:T(8,128)(2,1)} %copy-done.30, bf16[1536,256]{1,0:T(8,128)(2,1)} %copy-done.96, bf16[1536,256]{1,0:T(8,128)(2,1)} %copy-done.95, bf16[1536,256]{1,0:T(8,128)(2,1)} %copy-done.94, ...), custom_call_target="tpu_custom_call" | custom-call | flops 12884901888 | bytes 30416896 | tf_op jit(solution)/shard_map/join/pallas_call | solution.py:449
  404.7 22.0 %units.2 = (bf16[1536,768]{1,0:T(8,128)(2,1)}, bf16[1536,768]{1,0:T(8,128)(2,1)}, bf16[1536,768]{1,0:T(8,128)(2,1)}) custom-call(bf16[1536,2048]{1,0:T(8,128)(2,1)} %get-tuple-element.84.hb.refs_8_, bf16[1536,2048]{1,0:T(8,128)(2,1)} %constant_dynamic-update-slice_fusion.10.cot, bf16[2048,768]{1,0:T(8,128)(2,1)} %select_dynamic-update-slice_fusion.6.w_gate.refs_4_, ...), custom_call_target="tpu_custom_call" | custom-call | flops 14495514624 | bytes 29097984 | tf_op jit(solution)/shard_map/units/pallas_call | solution.py:449
  426.7 22.0 %units.3 = (bf16[1536,768]{1,0:T(8,128)(2,1)}, bf16[1536,768]{1,0:T(8,128)(2,1)}, bf16[1536,768]{1,0:T(8,128)(2,1)}) custom-call(bf16[1536,2048]{1,0:T(8,128)(2,1)} %get-tuple-element.84.hb.refs_8_, bf16[1536,2048]{1,0:T(8,128)(2,1)} %constant_dynamic-update-slice_fusion.10.cot, bf16[2048,768]{1,0:T(8,128)(2,1)} %collective-permute-done.62.w_gate.refs_6_, ...), custom_call_target="tpu_custom_call" | custom-call | flops 14495514624 | bytes 29097984 | tf_op jit(solution)/shard_map/units/pallas_call | solution.py:449
  448.7 17.2 %down.1 = (bf16[384,2048]{1,0:T(8,128)(2,1)}, bf16[2,384,1024]{2,1,0:T(8,128)(2,1)}, bf16[2,384,1024]{2,1,0:T(8,128)(2,1)}, bf16[384,1024]{1,0:T(8,128)(2,1)}, bf16[384,1024]{1,0:T(8,128)(2,1)}) custom-call(bf16[1536,768]{1,0:T(8,128)(2,1)} %get-tuple-element.89.m_own, bf16[1536,768]{1,0:T(8,128)(2,1)} %get-tuple-element.90.m_sis, ...), custom_call_target="tpu_custom_call" | custom-call | flops 9663676416 | bytes 17301504 | tf_op jit(solution)/shard_map/down/pallas_call | solution.py:449
  467.7 31.6 %grad_hb.1 = (bf16[384,2048]{1,0:T(8,128)(2,1)}, bf16[2,384,1024]{2,1,0:T(8,128)(2,1)}, bf16[2,384,1024]{2,1,0:T(8,128)(2,1)}, bf16[384,1024]{1,0:T(8,128)(2,1)}...) custom-call(bf16[1536,768]{1,0:T(8,128)(2,1)} %get-tuple-element.96.refs_0_, bf16[1536,768]{1,0:T(8,128)(2,1)} %get-tuple-element.97.refs_1_, ...), custom_call_target="tpu_custom_call" | custom-call | flops 19327352832 | bytes 34611200 | tf_op jit(solution)/shard_map/grad_hb/pallas_call | solution.py:449
  527.4 18.5 %collective-permute-done.70.from_y = bf16[2,384,1024]{2,1,0:T(8,128)(2,1)S(1)} collective-permute-done((bf16[2,384,1024]{2,1,0:T(8,128)(2,1)S(1)}, bf16[2,384,1024]{2,1,0:T(8,128)(2,1)S(1)}, u32[]{:S(2)}, u32[]{:S(2)}) %collective-permute-start.70) | collective-permute-done | bytes 1572896 | tf_op jit(solution)/shard_map/ppermute | solution.py:420
  558.2 21.0 %collective-permute-done.72.last_a = bf16[384,1024]{1,0:T(8,128)(2,1)S(1)} collective-permute-done((bf16[384,1024]{1,0:T(8,128)(2,1)S(1)}, bf16[384,1024]{1,0:T(8,128)(2,1)S(1)}, u32[]{:S(2)}, u32[]{:S(2)}) %collective-permute-start.72) | collective-permute-done | bytes 786464 | tf_op jit(solution)/shard_map/ppermute | solution.py:412
  580.4 11.9 %turn.1 = (f32[384,2048]{1,0:T(8,128)}, bf16[384,1024]{1,0:T(8,128)(2,1)}, bf16[384,1024]{1,0:T(8,128)(2,1)}, bf16[384,512]{1,0:T(8,128)(2,1)}, bf16[384,512]{1,...) custom-call(bf16[384,2048]{1,0:T(8,128)(2,1)} %get-tuple-element.100.own, ...), custom_call_target="tpu_custom_call" | custom-call | flops 3221225472 | bytes 30416896 | tf_op jit(solution)/shard_map/turn/pallas_call | solution.py:449
  687.9 25.1 %maximum_maximum_fusion = bf16[1536,2048]{1,0:T(8,128)(2,1)S(1)} fusion(bf16[384,1024]{1,0:T(8,128)(2,1)S(1)} %collective-permute-done.107, bf16[384,1024]{1,0:T(8,128)(2,1)S(1)} %collective-permute-done.106, bf16[384,1024]{1,0:T(8,128)(2,1)S(1)} %collective-permute-done.105, bf16[384,1024]{1,0:T(8,128)(2,1)S(1)} %copy-done.56, ...), kind=kLoop, calls=%fused_computation.1 | loop fusion | flops 50331648 | bytes 12582912 | tf_op jit(solution)/shard_map/concatenate | solution.py:1257
  718.4 42.8 %attend_back.1 = (bf16[1536,640]{1,0:T(8,128)(2,1)}, bf16[1536,640]{1,0:T(8,128)(2,1)}) custom-call(s32[7,24]{1,0:T(8,128)} %stack.26.tab, bf16[1536,640]{1,0:T(8,128)(2,1)} %copy-done.68, bf16[1536,640]{1,0:T(8,128)(2,1)} %copy-done.69, bf16[1536,256]{1,0:T(8,128)(2,1)} %get-tuple-element.80.refs_0_.refs_2_, bf16[1536,256]{1,0:T(8,128)(2,1)} %get-tuple-element.81.refs_3_, ...), custom_call_target="tpu_custom_call" | custom-call | flops 10066329600 | bytes 11010720 | tf_op jit(solution)/shard_map/attend_back/pallas_call | solution.py:449
  799.3 23.6 %heads_back.1 = (bf16[384,2048]{1,0:T(8,128)(2,1)}, bf16[2,384,1024]{2,1,0:T(8,128)(2,1)}, bf16[2,384,1024]{2,1,0:T(8,128)(2,1)}, bf16[384,1024]{1,0:T(8,128)(2,...) custom-call(bf16[1536,640]{1,0:T(8,128)(2,1)} %get-tuple-element.110, ...), custom_call_target="tpu_custom_call" | custom-call | flops 7247757312 | bytes 31074304 | tf_op jit(solution)/shard_map/heads_back/pallas_call | solution.py:449
  846.1 15.3 %collective-permute-start.121 = (bf16[512,768]{1,0:T(8,128)(2,1)S(1)}, bf16[512,768]{1,0:T(8,128)(2,1)S(1)}, u32[]{:S(2)}, u32[]{:S(2)}) collective-permute-start(bf16[512,768]{1,0:T(8,128)(2,1)S(1)} %get-tuple-element.154), channel_id=1, source_target_pairs={{0,8},{8,16},{16,24},{1,9},{9,17},{17,25},{2,10},{10,18},{18,26},{... | collective-permute-start | bytes 2359304 | tf_op jit(solution)/shard_map/ppermute | solution.py:865
  869.8 29.6 %collective-permute-done.111 = bf16[256,512]{1,0:T(8,128)(2,1)S(1)} collective-permute-done((bf16[256,512]{1,0:T(8,128)(2,1)S(1)}, bf16[256,512]{1,0:T(8,128)(2,1)S(1)}, u32[]{:S(2)}, u32[]{:S(2)}) %collective-permute-start.111) | collective-permute-done | bytes 262176 | tf_op jit(solution)/shard_map/ppermute | solution.py:865
  964.2 10.6 collective-permute-done.144
  991.7 10.2 collective-permute-done.85.last_b
  (684 shorter events, 631.9 us)
Async XLA Ops:
  12.8 60.1 %collective-permute-start.6 = (bf16[512,512]{1,0:T(8,128)(2,1)}, bf16[512,512]{1,0:T(8,128)(2,1)}, u32[]{:S(2)}, u32[]{:S(2)}) collective-permute-start(bf16[512,512]{1,0:T(8,128)(2,1)} %get-tuple-element.176), channel_id=1, source_target_pairs={{0,8},{8,16},{16,24},{1,9},{9,17},{17,25},{2,10},{10,18},{18,26},{... | collective-permute-start | bytes 1572872 | tf_op jit(solution)/shard_map/ppermute | solution.py:832
  18.1 54.8 %collective-permute-start.9 = (bf16[512,512]{1,0:T(8,128)(2,1)}, bf16[512,512]{1,0:T(8,128)(2,1)}, u32[]{:S(2)}, u32[]{:S(2)}) collective-permute-start(bf16[512,512]{1,0:T(8,128)(2,1)} %get-tuple-element.176), channel_id=1, source_target_pairs={{8,0},{16,8},{24,16},{9,1},{17,9},{25,17},{10,2},{18,10},{26,18},{... | collective-permute-start | bytes 1572872 | tf_op jit(solution)/shard_map/ppermute | solution.py:833
  148.4 61.4 %collective-permute-start.12 = (bf16[2048,512]{1,0:T(8,128)(2,1)}, bf16[2048,512]{1,0:T(8,128)(2,1)S(1)}, u32[]{:S(2)}, u32[]{:S(2)}) collective-permute-start(bf16[2048,512]{1,0:T(8,128)(2,1)} %select_dynamic-update-slice_fusion.9.w_own), channel_id=1, source_target_pairs={{0,2},{2,0},{4,6},{6,4},{1,3},{3,1},{5,7},{7,5},{8,10},{10,8},{12,... | collective-permute-start | bytes 6291464 | tf_op jit(solution)/shard_map/ppermute | solution.py:416
  350.5 76.2 %collective-permute-start.62 = (bf16[2048,768]{1,0:T(8,128)(2,1)}, bf16[2048,768]{1,0:T(8,128)(2,1)}, u32[]{:S(2)}, u32[]{:S(2)}) collective-permute-start(bf16[2048,768]{1,0:T(8,128)(2,1)} %select_dynamic-update-slice_fusion.6.w_gate.refs_4_), channel_id=1, source_target_pairs={{0,2},{2,0},{4,6},{6,4},{1,3},{3,1},{5,7},{7,5},{8,10},{10,8},{12,... | collective-permute-start | bytes 9437192 | tf_op jit(solution)/shard_map/ppermute | solution.py:416
  350.5 76.1 %collective-permute-start.63 = (bf16[2048,768]{1,0:T(8,128)(2,1)}, bf16[2048,768]{1,0:T(8,128)(2,1)}, u32[]{:S(2)}, u32[]{:S(2)}) collective-permute-start(bf16[2048,768]{1,0:T(8,128)(2,1)} %select_dynamic-update-slice_fusion.3.w_up.refs_5_), channel_id=1, source_target_pairs={{0,2},{2,0},{4,6},{6,4},{1,3},{3,1},{5,7},{7,5},{8,10},{10,8},{12,... | collective-permute-start | bytes 9437192 | tf_op jit(solution)/shard_map/ppermute | solution.py:416
  365.3 61.4 %collective-permute-start.64 = (bf16[768,2048]{1,0:T(8,128)(2,1)}, bf16[768,2048]{1,0:T(8,128)(2,1)}, u32[]{:S(2)}, u32[]{:S(2)}) collective-permute-start(bf16[768,2048]{1,0:T(8,128)(2,1)} %select_dynamic-update-slice_fusion.w_down.w_own), channel_id=1, source_target_pairs={{0,2},{2,0},{4,6},{6,4},{1,3},{3,1},{5,7},{7,5},{8,10},{10,8},{12,... | collective-permute-start | bytes 9437192 | tf_op jit(solution)/shard_map/ppermute | solution.py:416
  466.2 58.5 %collective-permute-start.67 = (bf16[2,384,1024]{2,1,0:T(8,128)(2,1)}, bf16[2,384,1024]{2,1,0:T(8,128)(2,1)}, u32[]{:S(2)}, u32[]{:S(2)}) collective-permute-start(bf16[2,384,1024]{2,1,0:T(8,128)(2,1)} %get-tuple-element.94), channel_id=1, source_target_pairs={{0,4},{4,0},{2,6},{6,2},{1,5},{5,1},{3,7},{7,3},{8,12},{12,8},{10,... | collective-permute-start | bytes 4718600 | tf_op jit(solution)/shard_map/ppermute | solution.py:412
  510.8 119.6 %collective-permute-start.118 = (bf16[2048,768]{1,0:T(8,128)(2,1)}, bf16[2048,768]{1,0:T(8,128)(2,1)}, u32[]{:S(2)}, u32[]{:S(2)}) collective-permute-start(bf16[2048,768]{1,0:T(8,128)(2,1)} %convolution_convert_fusion.2), channel_id=1, source_target_pairs={{0,2},{2,0},{4,6},{6,4},{1,3},{3,1},{5,7},{7,5},{8,10},{10,8},{12,... | collective-permute-start | bytes 9437192 | tf_op jit(solution)/shard_map/ppermute | solution.py:416
  523.1 69.1 %collective-permute-start.66 = (bf16[384,1024]{1,0:T(8,128)(2,1)}, bf16[384,1024]{1,0:T(8,128)(2,1)}, u32[]{:S(2)}, u32[]{:S(2)}) collective-permute-start(bf16[384,1024]{1,0:T(8,128)(2,1)} %fusion.8), channel_id=1, source_target_pairs={{0,4},{4,0},{2,6},{6,2},{1,5},{5,1},{3,7},{7,3},{8,12},{12,8},{10,... | collective-permute-start | bytes 2359304 | tf_op jit(solution)/shard_map/ppermute | solution.py:412
  527.1 65.7 %collective-permute-start.68 = (bf16[384,1024]{1,0:T(8,128)(2,1)}, bf16[384,1024]{1,0:T(8,128)(2,1)}, u32[]{:S(2)}, u32[]{:S(2)}) collective-permute-start(bf16[384,1024]{1,0:T(8,128)(2,1)} %fusion.6), channel_id=1, source_target_pairs={{0,1},{1,0},{2,3},{3,2},{4,5},{5,4},{6,7},{7,6},{8,9},{9,8},{10,11... | collective-permute-start | bytes 2359304 | tf_op jit(solution)/shard_map/ppermute | solution.py:420
  579.2 60.2 %collective-permute-start.128 = (bf16[2048,768]{1,0:T(8,128)(2,1)}, bf16[2048,768]{1,0:T(8,128)(2,1)}, u32[]{:S(2)}, u32[]{:S(2)}) collective-permute-start(bf16[2048,768]{1,0:T(8,128)(2,1)} %convolution_convert_fusion.1), channel_id=1, source_target_pairs={{0,2},{2,0},{4,6},{6,4},{1,3},{3,1},{5,7},{7,5},{8,10},{10,8},{12,... | collective-permute-start | bytes 9437192 | tf_op jit(solution)/shard_map/ppermute | solution.py:416
  579.2 73.1 %collective-permute-start.138 = (bf16[768,2048]{1,0:T(8,128)(2,1)}, bf16[768,2048]{1,0:T(8,128)(2,1)}, u32[]{:S(2)}, u32[]{:S(2)}) collective-permute-start(bf16[768,2048]{1,0:T(8,128)(2,1)} %convolution_convert_fusion), channel_id=1, source_target_pairs={{0,2},{2,0},{4,6},{6,4},{1,3},{3,1},{5,7},{7,5},{8,10},{10,8},{12,... | collective-permute-start | bytes 9437192 | tf_op jit(solution)/shard_map/ppermute | solution.py:416
  678.5 89.1 %collective-permute-start.132 = (bf16[512,768]{1,0:T(8,128)(2,1)}, bf16[512,768]{1,0:T(8,128)(2,1)}, u32[]{:S(2)}, u32[]{:S(2)}) collective-permute-start(bf16[512,768]{1,0:T(8,128)(2,1)} %get-tuple-element.153), channel_id=1, source_target_pairs={{24,16},{25,17},{26,18},{27,19},{28,20},{29,21},{30,22},{31,23}} | collective-permute-start | bytes 2359304 | tf_op jit(solution)/shard_map/ppermute | solution.py:862
  680.0 81.2 %collective-permute-start.139 = (bf16[768,512]{1,0:T(8,128)(2,1)}, bf16[768,512]{1,0:T(8,128)(2,1)}, u32[]{:S(2)}, u32[]{:S(2)}) collective-permute-start(bf16[768,512]{1,0:T(8,128)(2,1)} %get-tuple-element.148), channel_id=1, source_target_pairs={{0,8},{1,9},{2,10},{3,11},{4,12},{5,13},{6,14},{7,15}} | collective-permute-start | bytes 2359304 | tf_op jit(solution)/shard_map/ppermute | solution.py:861
  685.7 77.7 %collective-permute-start.120 = (bf16[512,768]{1,0:T(8,128)(2,1)S(1)}, bf16[512,768]{1,0:T(8,128)(2,1)}, u32[]{:S(2)}, u32[]{:S(2)}) collective-permute-start(bf16[512,768]{1,0:T(8,128)(2,1)S(1)} %add_convert_fusion.18), channel_id=1, source_target_pairs={{0,8},{8,16},{1,9},{9,17},{2,10},{10,18},{3,11},{11,19},{4,12},{12... | collective-permute-start | bytes 2359304 | tf_op jit(solution)/shard_map/ppermute | solution.py:863
  718.2 55.4 %collective-permute-start.108 = (bf16[256,2048]{1,0:T(8,128)(2,1)}, bf16[256,2048]{1,0:T(8,128)(2,1)S(1)}, u32[]{:S(2)}, u32[]{:S(2)}) collective-permute-start(bf16[256,2048]{1,0:T(8,128)(2,1)} %convolution_convert_fusion.4), channel_id=1, source_target_pairs={{0,2},{2,0},{4,6},{6,4},{1,3},{3,1},{5,7},{7,5},{8,10},{10,8},{12,... | collective-permute-start | bytes 3145736 | tf_op jit(solution)/shard_map/ppermute | solution.py:416
  769.0 73.2 %collective-permute-start.123 = (bf16[512,768]{1,0:T(8,128)(2,1)}, bf16[512,768]{1,0:T(8,128)(2,1)}, u32[]{:S(2)}, u32[]{:S(2)}) collective-permute-start(bf16[512,768]{1,0:T(8,128)(2,1)} %get-tuple-element.155), channel_id=1, source_target_pairs={{16,8},{24,16},{17,9},{25,17},{18,10},{26,18},{19,11},{27,19},{20,... | collective-permute-start | bytes 2359304 | tf_op jit(solution)/shard_map/ppermute | solution.py:864
  774.6 68.3 %collective-permute-start.133 = (bf16[512,768]{1,0:T(8,128)(2,1)}, bf16[512,768]{1,0:T(8,128)(2,1)}, u32[]{:S(2)}, u32[]{:S(2)}) collective-permute-start(bf16[512,768]{1,0:T(8,128)(2,1)} %get-tuple-element.151), channel_id=1, source_target_pairs={{16,8},{24,16},{17,9},{25,17},{18,10},{26,18},{19,11},{27,19},{20,... | collective-permute-start | bytes 2359304 | tf_op jit(solution)/shard_map/ppermute | solution.py:864
  837.4 83.5 %collective-permute-start.92 = (bf16[2048,512]{1,0:T(8,128)(2,1)S(1)}, bf16[2048,512]{1,0:T(8,128)(2,1)S(1)}, u32[]{:S(2)}, u32[]{:S(2)}) collective-permute-start(bf16[2048,512]{1,0:T(8,128)(2,1)S(1)} %convolution_convert_fusion.3), channel_id=1, source_target_pairs={{0,2},{2,0},{4,6},{6,4},{1,3},{3,1},{5,7},{7,5},{8,10},{10,8},{12,... | collective-permute-start | bytes 6291464 | tf_op jit(solution)/shard_map/ppermute | solution.py:416
  841.8 71.9 %collective-permute-start.69 = (bf16[384,2048]{1,0:T(8,128)(2,1)S(1)}, bf16[384,2048]{1,0:T(8,128)(2,1)S(1)}, u32[]{:S(2)}, u32[]{:S(2)}) collective-permute-start(bf16[384,2048]{1,0:T(8,128)(2,1)S(1)} %copy-done.15), channel_id=1, source_target_pairs={{0,1},{1,0},{2,3},{3,2},{4,5},{5,4},{6,7},{7,6},{8,9},{9,8},{10,11... | collective-permute-start | bytes 4718600 | tf_op jit(solution)/shard_map/ppermute | solution.py:420
  846.1 71.5 %collective-permute-start.121 = (bf16[512,768]{1,0:T(8,128)(2,1)S(1)}, bf16[512,768]{1,0:T(8,128)(2,1)S(1)}, u32[]{:S(2)}, u32[]{:S(2)}) collective-permute-start(bf16[512,768]{1,0:T(8,128)(2,1)S(1)} %get-tuple-element.154), channel_id=1, source_target_pairs={{0,8},{8,16},{16,24},{1,9},{9,17},{17,25},{2,10},{10,18},{18,26},{... | collective-permute-start | bytes 2359304 | tf_op jit(solution)/shard_map/ppermute | solution.py:865
  861.4 58.1 %collective-permute-start.131 = (bf16[512,768]{1,0:T(8,128)(2,1)S(1)}, bf16[512,768]{1,0:T(8,128)(2,1)S(1)}, u32[]{:S(2)}, u32[]{:S(2)}) collective-permute-start(bf16[512,768]{1,0:T(8,128)(2,1)S(1)} %copy-done.52), channel_id=1, source_target_pairs={{0,8},{8,16},{16,24},{1,9},{9,17},{17,25},{2,10},{10,18},{18,26},{... | collective-permute-start | bytes 2359304 | tf_op jit(solution)/shard_map/ppermute | solution.py:865
  917.7 60.2 %collective-permute-start.83 = (bf16[2,384,1024]{2,1,0:T(8,128)(2,1)S(1)}, bf16[2,384,1024]{2,1,0:T(8,128)(2,1)S(1)}, u32[]{:S(2)}, u32[]{:S(2)}) collective-permute-start(bf16[2,384,1024]{2,1,0:T(8,128)(2,1)S(1)} %copy-done.90), channel_id=1, source_target_pairs={{0,4},{4,0},{2,6},{6,2},{1,5},{5,1},{3,7},{7,3},{8,12},{12,8},{10,... | collective-permute-start | bytes 4718600 | tf_op jit(solution)/shard_map/ppermute | solution.py:412
  1011.4 57.4 %collective-permute-start.86 = (bf16[384,2048]{1,0:T(8,128)(2,1)}, bf16[384,2048]{1,0:T(8,128)(2,1)}, u32[]{:S(2)}, u32[]{:S(2)}) collective-permute-start(bf16[384,2048]{1,0:T(8,128)(2,1)} %get-tuple-element.125), channel_id=1, source_target_pairs={{0,1},{1,0},{2,3},{3,2},{4,5},{5,4},{6,7},{7,6},{8,9},{9,8},{10,11... | collective-permute-start | bytes 4718600 | tf_op jit(solution)/shard_map/ppermute | solution.py:420
  (239 other events, 5112.8 us)
